TPU v7x, 32 devices: a whole 2x2x4 slice. The times are simulated.
32 devices in a mesh: bearing: 8 (over z, x), freq: 4 (over y, core).
Axes of the slice: x: 2, y: 2, z: 4, core: 2. Of those that a mesh axis runs over, the one named last changes fastest.
Arguments:
- starter: bfloat16 [4, 2, 256, 1024], P('freq', None, 'bearing'), may hold values from -6 to 6
- propagator: bfloat16 [4, 2, 1024, 1024], P('freq'), may hold values from -1 to 1
- wavenumber: float32 [4], P('freq'), may hold values from 0.5 to 2
- sediment_loss: float32 [4], P('freq'), may hold values from 0.1 to 1
- env_speed: bfloat16 [256, 1024], P('bearing'), may hold values from -6 to 6
- bottom: int32 [256], P('bearing'), may hold values from 256 to 1023
- track_column: int32 [256, 24], P('bearing'), may hold values from 0 to 255
Outputs:
- band_power: float32 [256, 128], P(('bearing', 'freq'))
All inputs are finite; a program needn't handle non-finite values.
Results may differ from a plain program's by a relative error of at most 0.0011.
Values may be sent and summed in bfloat16 or wider, within the bound.
No kernel may reach another device: no remote copies, remote signals or barrier semaphores. Data moves between devices by JAX's collectives and lax.ppermute only.
A program may use at most 64 MiB of HBM per device.

v0:
```python
import jax
import jax.numpy as jnp
from jax import lax
from jax.sharding import PartitionSpec as P

BAND_CELLS = 8


def on_device(starter, propagator, wavenumber, sediment_loss, env_speed, bottom, track_column):
    bearings_here = track_column.shape[0]
    depth_cells = env_speed.shape[1]
    band_count = depth_cells // BAND_CELLS
    gathered, bottoms_all = (
        lax.all_gather(env_speed, "bearing", axis=0, tiled=True),
        lax.all_gather(bottom, "bearing", axis=0, tiled=True),
    )
    column_total = gathered.shape[0]
    depth_index = jnp.arange(depth_cells, dtype=jnp.int32)
    prop_re = propagator[0, 0]
    prop_im = propagator[0, 1]
    wavenum = wavenumber[0]
    decay = jnp.exp(-sediment_loss[0])

    def advance(carried, columns):
        mixed_re = jnp.dot(carried, prop_re, preferred_element_type=jnp.float32)
        mixed_im = jnp.dot(carried, prop_im, preferred_element_type=jnp.float32)
        moved_re = mixed_re[:bearings_here] - mixed_im[bearings_here:]
        moved_im = mixed_im[:bearings_here] + mixed_re[bearings_here:]
        sounds = gathered[columns].astype(jnp.float32)
        phases = wavenum * sounds
        deep_cells = depth_index[None, :] >= bottoms_all[columns][:, None]
        damping = jnp.where(deep_cells, decay, jnp.float32(1.0))
        cosine = jnp.cos(phases)
        sine = jnp.sin(phases)
        screened_re = (moved_re * cosine - moved_im * sine) * damping
        screened_im = (moved_re * sine + moved_im * cosine) * damping
        squared = screened_re * screened_re + screened_im * screened_im
        powers = squared.reshape(bearings_here, band_count, BAND_CELLS).sum(-1)
        following = jnp.concatenate([screened_re, screened_im], axis=0).astype(jnp.bfloat16)
        return (following, powers)

    initial = starter[0].reshape(2 * bearings_here, depth_cells)
    final_field, powers = lax.scan(advance, initial, track_column.T)
    steps_here = track_column.shape[1]
    targets = track_column.T.reshape(-1)
    grid = jax.ops.segment_sum(powers.reshape(-1, band_count), targets, num_segments=column_total)
    summed = lax.psum_scatter(grid, ("bearing", "freq"), scatter_dimension=0, tiled=True)
    bearing_total = bearings_here * lax.axis_size("bearing")
    freq_total = lax.axis_size("freq")
    return summed * (column_total / (bearing_total * steps_here * freq_total))


def solution(mesh):
    in_specs = (
        P("freq", None, "bearing", None),
        P("freq", None, None, None),
        P("freq"),
        P("freq"),
        P("bearing", None),
        P("bearing"),
        P("bearing", None),
    )
    out_specs = P(("bearing", "freq"), None)
    return jax.shard_map(
        on_device, mesh=mesh, in_specs=in_specs, out_specs=out_specs, check_vma=False
    )
```

profile of v0, /device:TPU:0, one launch (start us, length us, event | category | flops | bytes accessed | tf_op | source)
XLA Modules:
  0.0 342.3 jit_solution(10462708742214539513)
XLA Ops:
  6.6 4.1 %slice_bitcast_fusion = (bf16[1024,1024]{1,0:T(8,128)(2,1)S(1)}, bf16[1024,1024]{1,0:T(8,128)(2,1)}) fusion(bf16[1,2,1024,1024]{3,2,1,0:T(8,128)(2,1)} %param.10), kind=kLoop, calls=%fused_computation.19 | loop fusion | bytes 8388608 | tf_op jit(solution)/shard_map/squeeze | solution.py:20
  12.2 13.1 %all-reduce = s32[256]{0:T(256)S(1)} all-reduce(s32[256]{0:T(256)S(1)} %dynamic-update-slice), channel_id=1, replica_groups=mesh['bearing'=8,'freq'=4] {'bearing'}, use_global_device_ids=true, to_apply=%add | all-reduce | flops 256 | bytes 2048
  25.3 31.5 %all_gather.6 = bf16[256,1024]{1,0:T(8,128)(2,1)S(1)} all-gather(bf16[32,1024]{1,0:T(8,128)(2,1)S(1)} %copy-done.1), channel_id=1, replica_groups=mesh['bearing'=8,'freq'=4] {'bearing'}, dimensions={0}, use_global_device_ids=true | all-gather | bytes 589824 | tf_op jit(solution)/shard_map/all_gather | solution.py:14
  57.6 148.7 %while.13 = (s32[]{:T(128)}, bf16[64,1024]{1,0:T(8,128)(2,1)S(1)}, f32[24,32,128]{2,1,0:T(8,128)}, bf16[1024,1024]{1,0:T(8,128)(2,1)}, bf16[1024,1024]{1,0:T(8,1...) while((s32[]{:T(128)}, bf16[64,1024]{1,0:T(8,128)(2,1)S(1)}, ...), condition=%wide.region_2.3_spmd.clone, body=%wide.region_0.2_spmd.clone.sunk | while | flops 269349984 | bytes 6706809 | solution.py:43
  58.9 2.1 fusion.25
  61.5 1.2 multiply_add_fusion.2
  65.1 2.1 fusion.25
  67.7 1.2 multiply_add_fusion.2
  71.3 2.1 fusion.25
  73.9 1.2 multiply_add_fusion.2
  77.5 2.1 fusion.25
  80.1 1.2 multiply_add_fusion.2
  83.7 2.1 fusion.25
  86.3 1.2 multiply_add_fusion.2
  89.9 2.1 fusion.25
  92.5 1.2 multiply_add_fusion.2
  96.1 2.1 fusion.25
  98.7 1.2 multiply_add_fusion.2
  102.3 2.1 fusion.25
  104.9 1.2 multiply_add_fusion.2
  108.5 2.1 fusion.25
  111.0 1.2 multiply_add_fusion.2
  114.7 2.1 fusion.25
  117.2 1.2 multiply_add_fusion.2
  120.9 2.1 fusion.25
  123.4 1.2 multiply_add_fusion.2
  127.1 2.1 fusion.25
  133.3 2.1 fusion.25
  139.5 2.1 fusion.25
  145.6 2.1 fusion.25
  151.9 2.1 fusion.25
  154.4 1.2 multiply_add_fusion.2
  158.0 2.1 fusion.25
  164.2 2.1 fusion.25
  170.4 2.1 fusion.25
  173.0 1.2 multiply_add_fusion.2
  176.6 2.1 fusion.25
  179.2 1.2 multiply_add_fusion.2
  182.8 2.1 fusion.25
  185.4 1.2 multiply_add_fusion.2
  189.0 2.1 fusion.25
  195.2 2.1 fusion.25
  197.8 1.2 multiply_add_fusion.2
  201.4 2.1 fusion.25
  204.0 1.2 multiply_add_fusion.2
  206.3 7.0 %scatter_custom_fusion = f32[256,128]{1,0:T(8,128)} fusion(s32[768]{0:T(1024)S(1)} %reshape.57, f32[768,128]{1,0:T(8,128)} %bitcast.41, f32[]{:T(128)} %constant.4.clone.1), kind=kCustom, calls=%fused_computation.21 | custom fusion | flops 98304 | bytes 131584 | tf_op jit(solution)/shard_map/scatter-add | solution.py:46
  213.3 120.9 %all-reduce.4.cloned.1.call-done = f32[256,128]{1,0:T(8,128)} async-done(((f32[256,128]{1,0:T(8,128)}), f32[256,128]{1,0:T(8,128)}) %all-reduce.4.cloned.1.call-update) | async-done | bytes 131088
  334.2 1.3 dynamic-slice_multiply_fusion
  (264 shorter events, 78.5 us)
Async XLA Ops:
  6.5 327.7 %all-reduce.4.cloned.1.call-start = ((), (), s32[]{:S(2)}) async-start(), calls=%async_computation | async-start | bytes 262144
  6.5 4.1 %copy-start.4 = (u32[32]{0:T(128)S(1)}, u32[32]{0:T(128)}, u32[]{:S(2)}) copy-start(u32[32]{0:T(128)} %constant.29) | copy-start | bytes 388
  6.5 5.4 %copy-start.3 = (s32[32]{0:T(128)S(1)}, s32[32]{0:T(128)}, u32[]{:S(2)}) copy-start(s32[32]{0:T(128)} %param.14) | copy-start | bytes 388
  6.5 18.7 %copy-start.1 = (bf16[32,1024]{1,0:T(8,128)(2,1)S(1)}, bf16[32,1024]{1,0:T(8,128)(2,1)}, u32[]{:S(2)}) copy-start(bf16[32,1024]{1,0:T(8,128)(2,1)} %param.13) | copy-start | bytes 196612
  6.5 50.9 %copy-start.2 = (s32[32,24]{0,1:T(8,128)S(1)}, s32[32,24]{0,1:T(8,128)}, u32[]{:S(2)}) copy-start(s32[32,24]{0,1:T(8,128)} %param.15) | copy-start | bytes 9220
  6.6 51.0 %copy-start = (bf16[1,2,32,1024]{3,2,1,0:T(8,128)(2,1)S(1)}, bf16[1,2,32,1024]{3,2,1,0:T(8,128)(2,1)}, u32[]{:S(2)}) copy-start(bf16[1,2,32,1024]{3,2,1,0:T(8,128)(2,1)} %param.9) | copy-start | bytes 393220
Sparse Core Ops, SparseCore 0:
  213.4 120.7 all-reduce.3
where the time goes:
time: 344 us; the launch traced here: 342 us
  waiting for transfers between devices  121 us (35%)
  matrix products  61.4 us (18%)
  local copies, waits for them, and re-layouts  58.1 us (17%)
  blocking collectives  44.6 us (13%)
  other arithmetic  41.4 us (12%)
  between operations  14.8 us (4%)
    unnamed x2, waiting for transfers between devices  121 us
    dot_general x24, matrix products, advance(): mixed_re = jnp.dot(carried, prop_re, preferred_element_type=jnp.float32)  49.8 us
    all_gather x1, blocking collectives, on_device(): lax.all_gather(env_speed, 'bearing', axis=0, tiled=True)  31.5 us
    add x24, other arithmetic, advance(): squared = screened_re * screened_re + screened_im * screened_im  28.5 us
    gather x24, local copies, waits for them, and re-layouts, advance(): deep_cells = depth_index[None, :] >= bottoms_all[columns][:, None]  17 us
    dynamic_update_slice x48, local copies, waits for them, and re-layouts, on_device(): final_field, powers = lax.scan(advance, initial, track_column.T)  16.3 us
    gather x24, local copies, waits for them, and re-layouts, advance(): sounds = gathered[columns].astype(jnp.float32)  15.1 us
    unnamed x1, blocking collectives  13.1 us
  transfers between devices with their start and end apart: 1, of which 1 were waited for; matrix products, arithmetic and copies ran while one was open for 0% of the time, Pallas kernels for 0%

commit v1 on v0

v1 whole, which is shorter than its diff:
```python
import functools

import jax
import jax.numpy as jnp
from jax import lax
from jax.experimental import pallas as pl
from jax.experimental.pallas import tpu as pltpu
from jax.sharding import PartitionSpec as P

BAND_CELLS = 8
LANES = 128
CHUNK = 256
QUARTER_TURN = 0.6366197723675814
SIN_TERMS = (1.5707963219600276, -0.6459634781534198, 0.079680222858126, -0.004602163104811149)
COS_TERMS = (0.9999999723759501, -1.2336970108360321, 0.25359860771245774, -0.020408255467132635)


def polynomial(terms, square):
    total = jnp.float32(terms[-1])
    for term in terms[-2::-1]:
        total = total * square + jnp.float32(term)
    return total


def sine_and_cosine(turns):
    nearest = jnp.round(turns)
    rest = turns - nearest
    quadrant = nearest.astype(jnp.int32)
    square = rest * rest
    sine = polynomial(SIN_TERMS, square) * rest
    cosine = polynomial(COS_TERMS, square)
    odd = (quadrant & 1) != 0
    return (
        jnp.where(odd, cosine, sine),
        jnp.where(odd, sine, cosine),
        (quadrant & 2) != 0,
        ((quadrant + 1) & 2) != 0,
    )


def propagate(
    bands_of,
    track_smem, bottom_smem, scalars_smem, ids_ref, starter_ref, prop_ref, *rest,
):
    env_refs, (grid_ref, table, field_a, field_b, sin_a, cos_a, sin_b, cos_b, powers) = rest[:-9], rest[-9:]
    owner_total = len(env_refs)
    columns_here, depth_cells = env_refs[0].shape
    pieces = depth_cells // LANES
    steps, bearings = track_smem.shape
    column_total = grid_ref.shape[0]
    me = scalars_smem[2].astype(jnp.int32)
    per_turn = scalars_smem[0] * jnp.float32(QUARTER_TURN)
    decay = scalars_smem[1]

    for shift, env_ref in enumerate(env_refs):
        owner = lax.rem(me - shift + owner_total, owner_total)
        base = owner * (columns_here * pieces)
        for piece in range(pieces):
            block = env_ref[:, piece * LANES : (piece + 1) * LANES].astype(jnp.float32)
            table[pl.ds(base + piece, columns_here, stride=pieces), :] = block * per_turn
    field_a[...] = starter_ref[...]

    depth_index = lax.broadcasted_iota(jnp.int32, (pieces, LANES), 0) * LANES + lax.broadcasted_iota(
        jnp.int32, (pieces, LANES), 1
    )

    def prepare(step, sin_ref, cos_ref):
        for bearing in range(bearings):
            column = track_smem[step, bearing]
            turns = table[pl.ds(pl.multiple_of(column * pieces, pieces), pieces), :]
            sine, cosine, sine_minus, cosine_minus = sine_and_cosine(turns)
            damping = jnp.where(depth_index >= bottom_smem[column], decay, jnp.float32(1.0))
            rows = slice(bearing * pieces, (bearing + 1) * pieces)
            sin_ref[rows, :] = sine * jnp.where(sine_minus, -damping, damping)
            cos_ref[rows, :] = cosine * jnp.where(cosine_minus, -damping, damping)

    lane = lax.broadcasted_iota(jnp.int32, (bearings, LANES), 1)

    def fold(first, second, width):
        return jnp.where(
            (lane & width) == 0,
            first + pltpu.roll(first, LANES - width, 1),
            second + pltpu.roll(second, width, 1),
        )

    def advance(step, field, following, sin_ref, cos_ref):
        squares = []
        for start in range(0, depth_cells, CHUNK):
            cells = slice(start, start + CHUNK)
            mixed_re = jnp.dot(field[...], prop_ref[0, :, cells], preferred_element_type=jnp.float32)
            mixed_im = jnp.dot(field[...], prop_ref[1, :, cells], preferred_element_type=jnp.float32)
            moved_re = mixed_re[:bearings] - mixed_im[bearings:]
            moved_im = mixed_im[:bearings] + mixed_re[bearings:]
            for part in range(CHUNK // LANES):
                piece = start // LANES + part
                inner = slice(part * LANES, (part + 1) * LANES)
                outer = slice(piece * LANES, (piece + 1) * LANES)
                sine = sin_ref[pl.ds(piece, bearings, stride=pieces), :]
                cosine = cos_ref[pl.ds(piece, bearings, stride=pieces), :]
                screened_re = moved_re[:, inner] * cosine - moved_im[:, inner] * sine
                screened_im = moved_re[:, inner] * sine + moved_im[:, inner] * cosine
                following[:bearings, outer] = screened_re.astype(jnp.bfloat16)
                following[bearings:, outer] = screened_im.astype(jnp.bfloat16)
                squares.append(screened_re * screened_re + screened_im * screened_im)
        width = 1
        while len(squares) > 1:
            squares = [fold(squares[i], squares[i + 1], width) for i in range(0, len(squares), 2)]
            width *= 2
        rows = pl.ds(pl.multiple_of(step * bearings, bearings), bearings)
        powers[rows, :] = squares[0]

    prepare(0, sin_a, cos_a)

    def two_steps(pair, carry):
        step = pair * 2
        prepare(step + 1, sin_b, cos_b)
        advance(step, field_a, field_b, sin_a, cos_a)
        prepare(jnp.minimum(step + 2, steps - 1), sin_a, cos_a)
        advance(step + 1, field_b, field_a, sin_b, cos_b)
        return carry

    lax.fori_loop(0, steps // 2, two_steps, 0)

    tracks = steps * bearings
    chosen = (lax.broadcasted_iota(jnp.int32, (column_total, tracks), 0) == ids_ref[...]).astype(jnp.bfloat16)
    high = powers[...].astype(jnp.bfloat16)
    low = (powers[...] - high.astype(jnp.float32)).astype(jnp.bfloat16)
    both = jnp.dot(chosen, jnp.concatenate([high, low], axis=1), preferred_element_type=jnp.float32)
    grid_ref[...] = both[:, :LANES] + both[:, LANES:]


def finish(scale, parts_ref, out_ref):
    total = jnp.sum(parts_ref[...].astype(jnp.float32), axis=0) * jnp.float32(scale)
    row = lax.broadcasted_iota(jnp.int32, (LANES, LANES), 0)
    column = lax.broadcasted_iota(jnp.int32, (LANES, LANES), 1)
    groups = LANES // BAND_CELLS
    place = (row % BAND_CELLS) * groups + row // BAND_CELLS
    order = (place == column).astype(jnp.float32)
    out_ref[...] = jnp.dot(total, order, precision=lax.Precision.HIGHEST, preferred_element_type=jnp.float32)


def on_device(starter, propagator, wavenumber, sediment_loss, env_speed, bottom, track_column):
    bearings_here, steps = track_column.shape
    columns_here, depth_cells = env_speed.shape
    bands = depth_cells // BAND_CELLS
    owners = lax.axis_size("bearing")
    devices = owners * lax.axis_size("freq")
    column_total = columns_here * owners

    blocks = [env_speed] + [
        lax.ppermute(env_speed, "bearing", [(i, (i + shift) % owners) for i in range(owners)])
        for shift in range(1, owners)
    ]
    bottoms_all = lax.all_gather(bottom, "bearing", axis=0, tiled=True)
    tracks = track_column.T
    scalars = jnp.stack(
        [wavenumber[0], jnp.exp(-sediment_loss[0]), lax.axis_index("bearing").astype(jnp.float32)]
    )
    pieces = depth_cells // LANES
    smem = pl.BlockSpec(memory_space=pltpu.SMEM)
    vmem = pl.BlockSpec(memory_space=pltpu.VMEM)
    grid = pl.pallas_call(
        functools.partial(propagate, bands),
        out_shape=jax.ShapeDtypeStruct((column_total, bands), jnp.float32),
        in_specs=[smem] * 3 + [vmem] * (3 + len(blocks)),
        out_specs=vmem,
        scratch_shapes=[
            pltpu.VMEM((column_total * pieces, LANES), jnp.float32),
            pltpu.VMEM((2 * bearings_here, depth_cells), jnp.bfloat16),
            pltpu.VMEM((2 * bearings_here, depth_cells), jnp.bfloat16),
        ]
        + [pltpu.VMEM((bearings_here * pieces, LANES), jnp.float32)] * 4
        + [pltpu.VMEM((steps * bearings_here, bands), jnp.float32)],
        compiler_params=pltpu.CompilerParams(vmem_limit_bytes=40 * 1024 * 1024),
        name="propagate",
    )(
        tracks, bottoms_all, scalars, tracks.reshape(1, -1),
        starter[0].reshape(2 * bearings_here, depth_cells), propagator[0], *blocks,
    )
    parts = lax.all_to_all(
        grid.reshape(devices, column_total // devices, bands), ("bearing", "freq"), 0, 0
    )
    scale = column_total / (bearings_here * owners * steps * lax.axis_size("freq"))
    return pl.pallas_call(
        functools.partial(finish, scale),
        out_shape=jax.ShapeDtypeStruct((column_total // devices, bands), jnp.float32),
        in_specs=[vmem],
        out_specs=vmem,
        name="finish",
    )(parts)


def solution(mesh):
    in_specs = (
        P("freq", None, "bearing", None),
        P("freq", None, None, None),
        P("freq"),
        P("freq"),
        P("bearing", None),
        P("bearing"),
        P("bearing", None),
    )
    out_specs = P(("bearing", "freq"), None)
    return jax.shard_map(
        on_device, mesh=mesh, in_specs=in_specs, out_specs=out_specs, check_vma=False
    )
```

time: 344 us -> 81 us (0.24)
  waiting for transfers between devices: 121 us -> 2.37 us
  matrix products: 61.4 us -> 0 us
  local copies, waits for them, and re-layouts: 58.1 us -> 7.52 us
  other arithmetic: 41.4 us -> 0.08 us
  Pallas kernels: 0 us -> 28.8 us
  blocking collectives: 44.6 us -> 25.2 us
  starting transfers between devices: 0.01 us -> 14.6 us
  between operations: 14.8 us -> 2.02 us
    unnamed x2 -> x0, waiting for transfers between devices: 121 us -> none
    dot_general x48 -> x0, matrix products: 61.4 us -> none  [the longest x24 49.8 us: advance(): mixed_re = jnp.dot(carried, prop_re, preferred_element_type=jnp.float32)]
    gather x48 -> x0, local copies, waits for them, and re-layouts: 32.1 us -> none  [the longest x24 17 us: advance(): deep_cells = depth_index[None, :] >= bottoms_all[columns][:, None]]
    all_gather x1 -> x0, blocking collectives: 31.5 us -> none  [on_device(): lax.all_gather(env_speed, 'bearing', axis=0, tiled=True)]
    pallas_call x0 -> x2, Pallas kernels: none -> 28.8 us  [the longest x1 27.1 us: on_device(): pl.pallas_call(functools.partial(propagate, bands), out_shape=jax.ShapeDt...]
    add x24 -> x0, other arithmetic: 28.5 us -> none  [advance(): squared = screened_re * screened_re + screened_im * screened_im]
    dynamic_update_slice x48 -> x0, local copies, waits for them, and re-layouts: 16.3 us -> none  [on_device(): final_field, powers = lax.scan(advance, initial, track_column.T)]
    ppermute x0 -> x7, starting transfers between devices: none -> 14.6 us  [on_device(): lax.ppermute(env_speed, 'bearing', [(i, (i + shift) % owners) for i in ra...]
  transfers between devices with their start and end apart: 1 -> 7, of which waited for: 1 -> 1; matrix products, arithmetic and copies ran while one was open for 0% -> 4% of each run, Pallas kernels for 0% -> 0%
where the time goes in v1:
time: 81 us; the launch traced here: 80.6 us
  Pallas kernels  28.8 us (36%)
  blocking collectives  25.2 us (31%)
  starting transfers between devices  14.6 us (18%)
  local copies, waits for them, and re-layouts  7.52 us (9%)
  waiting for transfers between devices  2.37 us (3%)
  between operations  2.02 us (2%)
    pallas_call x1, Pallas kernels, on_device(): pl.pallas_call(functools.partial(propagate, bands), out_shape=jax.ShapeDt...  27.1 us
    ppermute x7, starting transfers between devices, on_device(): lax.ppermute(env_speed, 'bearing', [(i, (i + shift) % owners) for i in ra...  14.6 us
    all_to_all x1, blocking collectives, on_device(): lax.all_to_all(grid.reshape(devices, column_total // devices, bands), ('b...  14.2 us
    unnamed x1, blocking collectives  11 us
    unnamed x11, local copies, waits for them, and re-layouts  6.74 us
    ppermute x7, waiting for transfers between devices, on_device(): lax.ppermute(env_speed, 'bearing', [(i, (i + shift) % owners) for i in ra...  2.37 us
    pallas_call x1, Pallas kernels, on_device(): pl.pallas_call(functools.partial(finish, scale), out_shape=jax.ShapeDtype...  1.7 us
  transfers between devices with their start and end apart: 7, of which 1 were waited for; matrix products, arithmetic and copies ran while one was open for 4% of the time, Pallas kernels for 0%

profile of v1, /device:TPU:0, one launch (start us, length us, event | category | flops | bytes accessed | tf_op | source)
XLA Modules:
  0.0 80.6 jit_solution(4516720647440096100)
XLA Ops:
  0.0 5.0 %collective-permute-start.5 = (bf16[32,1024]{1,0:T(8,128)(2,1)}, bf16[32,1024]{1,0:T(8,128)(2,1)S(1)}, u32[]{:S(2)}, u32[]{:S(2)}) collective-permute-start(bf16[32,1024]{1,0:T(8,128)(2,1)} %rest_0_.1), channel_id=1, source_target_pairs={{0,24},{4,28},{8,0},{12,4},{16,8},{20,12},{24,16},{28,20},{1,25},{... | collective-permute-start | bytes 196616 | tf_op jit(solution)/shard_map/ppermute | solution.py:151
  5.0 0.4 collective-permute-start.4
  5.4 3.5 %collective-permute-start.3 = (bf16[32,1024]{1,0:T(8,128)(2,1)}, bf16[32,1024]{1,0:T(8,128)(2,1)S(1)}, u32[]{:S(2)}, u32[]{:S(2)}) collective-permute-start(bf16[32,1024]{1,0:T(8,128)(2,1)} %rest_0_.1), channel_id=1, source_target_pairs={{0,16},{4,20},{8,24},{12,28},{16,0},{20,4},{24,8},{28,12},{1,17},{... | collective-permute-start | bytes 196616 | tf_op jit(solution)/shard_map/ppermute | solution.py:151
  8.9 0.0 collective-permute-start.2
  8.9 1.0 %collective-permute-start.1 = (bf16[32,1024]{1,0:T(8,128)(2,1)}, bf16[32,1024]{1,0:T(8,128)(2,1)S(1)}, u32[]{:S(2)}, u32[]{:S(2)}) collective-permute-start(bf16[32,1024]{1,0:T(8,128)(2,1)} %rest_0_.1), channel_id=1, source_target_pairs={{0,8},{4,12},{8,16},{12,20},{16,24},{20,28},{24,0},{28,4},{1,9},{5... | collective-permute-start | bytes 196616 | tf_op jit(solution)/shard_map/ppermute | solution.py:151
  11.2 0.8 reshape.9.ids_ref
  12.0 1.2 %dynamic-slice = u32[1]{0:T(128)} dynamic-slice(u32[32]{0:T(128)} %constant.12, u32[]{:T(128)S(6)} %add), dynamic_slice_sizes={1} | dynamic-slice | bytes 12
  13.9 0.9 %dynamic-update-slice = s32[256]{0:T(256)S(1)} dynamic-update-slice(s32[256]{0:T(256)S(1)} %broadcast, s32[32]{0:T(128)} %param.12, u32[]{:T(128)} %bitcast.1) | dynamic-update-slice | bytes 260
  14.8 11.0 %all-reduce.bottom_smem = s32[256]{0:T(256)S(1)} all-reduce(s32[256]{0:T(256)S(1)} %dynamic-update-slice), channel_id=1, replica_groups=mesh['bearing'=8,'freq'=4] {'bearing'}, use_global_device_ids=true, to_apply=%add | all-reduce | flops 256 | bytes 2048
  25.7 0.0 collective-permute-done.5.rest_6_
  25.7 1.4 %collective-permute-start = (bf16[32,1024]{1,0:T(8,128)(2,1)}, bf16[32,1024]{1,0:T(8,128)(2,1)S(1)}, u32[]{:S(2)}, u32[]{:S(2)}) collective-permute-start(bf16[32,1024]{1,0:T(8,128)(2,1)} %rest_0_.1), channel_id=1, source_target_pairs={{0,4},{4,8},{8,12},{12,16},{16,20},{20,24},{24,28},{28,0},{1,5},{5... | collective-permute-start | bytes 196616 | tf_op jit(solution)/shard_map/ppermute | solution.py:151
  27.2 0.0 collective-permute-done.4.rest_5_
  27.2 3.3 %collective-permute-start.6 = (bf16[32,1024]{1,0:T(8,128)(2,1)}, bf16[32,1024]{1,0:T(8,128)(2,1)S(1)}, u32[]{:S(2)}, u32[]{:S(2)}) collective-permute-start(bf16[32,1024]{1,0:T(8,128)(2,1)} %rest_0_.1), channel_id=1, source_target_pairs={{0,28},{4,0},{8,4},{12,8},{16,12},{20,16},{24,20},{28,24},{1,29},{... | collective-permute-start | bytes 196616 | tf_op jit(solution)/shard_map/ppermute | solution.py:151
  30.5 0.1 pad_maximum_fusion.scalars_smem
  30.5 0.0 collective-permute-done.3.rest_4_
  30.5 0.0 collective-permute-done.2.rest_3_
  30.5 0.0 collective-permute-done.1.rest_2_
  30.5 2.4 %collective-permute-done.rest_1_ = bf16[32,1024]{1,0:T(8,128)(2,1)S(1)} collective-permute-done((bf16[32,1024]{1,0:T(8,128)(2,1)}, bf16[32,1024]{1,0:T(8,128)(2,1)S(1)}, u32[]{:S(2)}, u32[]{:S(2)}) %collective-permute-start) | collective-permute-done | bytes 65568 | tf_op jit(solution)/shard_map/ppermute | solution.py:151
  32.9 0.0 collective-permute-done.6.rest_7_
  32.9 0.0 copy-start
  32.9 2.2 %copy-done = bf16[1,2,1024,1024]{3,2,1,0:T(8,128)(2,1)S(1)} copy-done((bf16[1,2,1024,1024]{3,2,1,0:T(8,128)(2,1)S(1)}, bf16[1,2,1024,1024]{3,2,1,0:T(8,128)(2,1)}, u32[]{:S(2)}) %copy-start) | copy-done | bytes 4194328
  35.1 0.0 copy-start.1
  35.1 0.9 %copy-done.1 = bf16[1,2,32,1024]{3,2,1,0:T(8,128)(2,1)S(1)} copy-done((bf16[1,2,32,1024]{3,2,1,0:T(8,128)(2,1)S(1)}, bf16[1,2,32,1024]{3,2,1,0:T(8,128)(2,1)}, u32[]{:S(2)}) %copy-start.1) | copy-done | bytes 131096
  36.0 0.0 copy-start.2
  36.0 0.8 %copy-done.2 = bf16[32,1024]{1,0:T(8,128)(2,1)S(1)} copy-done((bf16[32,1024]{1,0:T(8,128)(2,1)S(1)}, bf16[32,1024]{1,0:T(8,128)(2,1)}, u32[]{:S(2)}) %copy-start.2) | copy-done | bytes 65560
  36.8 0.0 copy-start.3
  36.8 0.7 copy-done.3
  37.5 27.1 %propagate.1 = f32[256,128]{1,0:T(8,128)S(1)} custom-call(s32[24,32]{1,0:T(8,128)S(1)} %bitcast.10, s32[256]{0:T(256)S(1)} %all-reduce.bottom_smem, f32[3]{0:T(128)S(1)} %pad_maximum_fusion.scalars_smem, s32[1,768]{1,0:T(1,128)S(1)} %reshape.9.ids_ref, bf16[64,1024]{1,0:T(8,128)(2,1)S(1)} %bitcast.8, bf16[2,1024,1024]{2,1,0:T(8,128)(2,1)S(1)} %bitcast.6, ...), custom_call_target="tpu_custom_call" | custom-call | tf_op jit(solution)/shard_map/propagate/pallas_call | solution.py:162
  64.7 14.2 %all_to_all.5.parts_ref = f32[32,8,128]{2,1,0:T(8,128)} all-to-all(f32[32,8,128]{2,1,0:T(8,128)S(1)} %bitcast.7), channel_id=1, replica_groups=mesh['bearing'=8,'freq'=4] {'bearing','freq'}, dimensions={0} | all-to-all | bytes 262144 | tf_op jit(solution)/shard_map/all_to_all | solution.py:180
  78.9 1.7 %finish.1 = f32[8,128]{1,0:T(8,128)} custom-call(f32[32,8,128]{2,1,0:T(8,128)} %all_to_all.5.parts_ref), custom_call_target="tpu_custom_call" | custom-call | tf_op jit(solution)/shard_map/finish/pallas_call | solution.py:184
  (1 shorter events, 0.0 us)
Async XLA Ops:
  0.0 25.7 %collective-permute-start.5 = (bf16[32,1024]{1,0:T(8,128)(2,1)}, bf16[32,1024]{1,0:T(8,128)(2,1)S(1)}, u32[]{:S(2)}, u32[]{:S(2)}) collective-permute-start(bf16[32,1024]{1,0:T(8,128)(2,1)} %rest_0_.1), channel_id=1, source_target_pairs={{0,24},{4,28},{8,0},{12,4},{16,8},{20,12},{24,16},{28,20},{1,25},{... | collective-permute-start | bytes 196616 | tf_op jit(solution)/shard_map/ppermute | solution.py:151
  5.0 22.1 %collective-permute-start.4 = (bf16[32,1024]{1,0:T(8,128)(2,1)}, bf16[32,1024]{1,0:T(8,128)(2,1)S(1)}, u32[]{:S(2)}, u32[]{:S(2)}) collective-permute-start(bf16[32,1024]{1,0:T(8,128)(2,1)} %rest_0_.1), channel_id=1, source_target_pairs={{0,20},{4,24},{8,28},{12,0},{16,4},{20,8},{24,12},{28,16},{1,21},{... | collective-permute-start | bytes 196616 | tf_op jit(solution)/shard_map/ppermute | solution.py:151
  5.4 25.1 %collective-permute-start.3 = (bf16[32,1024]{1,0:T(8,128)(2,1)}, bf16[32,1024]{1,0:T(8,128)(2,1)S(1)}, u32[]{:S(2)}, u32[]{:S(2)}) collective-permute-start(bf16[32,1024]{1,0:T(8,128)(2,1)} %rest_0_.1), channel_id=1, source_target_pairs={{0,16},{4,20},{8,24},{12,28},{16,0},{20,4},{24,8},{28,12},{1,17},{... | collective-permute-start | bytes 196616 | tf_op jit(solution)/shard_map/ppermute | solution.py:151
  8.9 21.6 %collective-permute-start.2 = (bf16[32,1024]{1,0:T(8,128)(2,1)}, bf16[32,1024]{1,0:T(8,128)(2,1)S(1)}, u32[]{:S(2)}, u32[]{:S(2)}) collective-permute-start(bf16[32,1024]{1,0:T(8,128)(2,1)} %rest_0_.1), channel_id=1, source_target_pairs={{0,12},{4,16},{8,20},{12,24},{16,28},{20,0},{24,4},{28,8},{1,13},{... | collective-permute-start | bytes 196616 | tf_op jit(solution)/shard_map/ppermute | solution.py:151
  8.9 21.6 %collective-permute-start.1 = (bf16[32,1024]{1,0:T(8,128)(2,1)}, bf16[32,1024]{1,0:T(8,128)(2,1)S(1)}, u32[]{:S(2)}, u32[]{:S(2)}) collective-permute-start(bf16[32,1024]{1,0:T(8,128)(2,1)} %rest_0_.1), channel_id=1, source_target_pairs={{0,8},{4,12},{8,16},{12,20},{16,24},{20,28},{24,0},{28,4},{1,9},{5... | collective-permute-start | bytes 196616 | tf_op jit(solution)/shard_map/ppermute | solution.py:151
  25.7 7.2 %collective-permute-start = (bf16[32,1024]{1,0:T(8,128)(2,1)}, bf16[32,1024]{1,0:T(8,128)(2,1)S(1)}, u32[]{:S(2)}, u32[]{:S(2)}) collective-permute-start(bf16[32,1024]{1,0:T(8,128)(2,1)} %rest_0_.1), channel_id=1, source_target_pairs={{0,4},{4,8},{8,12},{12,16},{16,20},{20,24},{24,28},{28,0},{1,5},{5... | collective-permute-start | bytes 196616 | tf_op jit(solution)/shard_map/ppermute | solution.py:151
  27.2 5.7 %collective-permute-start.6 = (bf16[32,1024]{1,0:T(8,128)(2,1)}, bf16[32,1024]{1,0:T(8,128)(2,1)S(1)}, u32[]{:S(2)}, u32[]{:S(2)}) collective-permute-start(bf16[32,1024]{1,0:T(8,128)(2,1)} %rest_0_.1), channel_id=1, source_target_pairs={{0,28},{4,0},{8,4},{12,8},{16,12},{20,16},{24,20},{28,24},{1,29},{... | collective-permute-start | bytes 196616 | tf_op jit(solution)/shard_map/ppermute | solution.py:151
  32.9 2.2 %copy-start = (bf16[1,2,1024,1024]{3,2,1,0:T(8,128)(2,1)S(1)}, bf16[1,2,1024,1024]{3,2,1,0:T(8,128)(2,1)}, u32[]{:S(2)}) copy-start(bf16[1,2,1024,1024]{3,2,1,0:T(8,128)(2,1)} %param.8) | copy-start | bytes 12582916
  35.1 0.9 %copy-start.1 = (bf16[1,2,32,1024]{3,2,1,0:T(8,128)(2,1)S(1)}, bf16[1,2,32,1024]{3,2,1,0:T(8,128)(2,1)}, u32[]{:S(2)}) copy-start(bf16[1,2,32,1024]{3,2,1,0:T(8,128)(2,1)} %param.7) | copy-start | bytes 393220
  36.0 0.8 %copy-start.2 = (bf16[32,1024]{1,0:T(8,128)(2,1)S(1)}, bf16[32,1024]{1,0:T(8,128)(2,1)}, u32[]{:S(2)}) copy-start(bf16[32,1024]{1,0:T(8,128)(2,1)} %rest_0_.1) | copy-start | bytes 196612
  36.8 0.7 copy-start.3

commit v2 on v1

v2 whole, which is shorter than its diff:
```python
import functools

import jax
import jax.numpy as jnp
from jax import lax
from jax.experimental import pallas as pl
from jax.experimental.pallas import tpu as pltpu
from jax.sharding import PartitionSpec as P

BAND_CELLS = 8
LANES = 128
TILE = 256
PAD_ROWS = 64
EXTRA_ROWS = 16
CODE_BASE = 256
QUARTER_TURN = 0.6366197723675814
SIN_TERMS = (1.5707963219600276, -0.6459634781534198, 0.079680222858126, -0.004602163104811149)
COS_TERMS = (0.9999999723759501, -1.2336970108360321, 0.25359860771245774, -0.020408255467132635)
VMEM_LIMIT = 60 * 1024 * 1024


def polynomial(terms, square):
    total = jnp.float32(terms[-1])
    for term in terms[-2::-1]:
        total = total * square + jnp.float32(term)
    return total


def sine_and_cosine(turns):
    nearest = jnp.round(turns)
    rest = turns - nearest
    quadrant = nearest.astype(jnp.int32)
    square = rest * rest
    sine = polynomial(SIN_TERMS, square) * rest
    cosine = polynomial(COS_TERMS, square)
    odd = (quadrant & 1) != 0
    return (
        jnp.where(odd, cosine, sine),
        jnp.where(odd, sine, cosine),
        (quadrant & 2) != 0,
        ((quadrant + 1) & 2) != 0,
    )


def pack(env_ref, bottom_ref, out_ref, wide):
    columns, depth_cells = env_ref.shape
    pieces = depth_cells // LANES
    for piece in range(pieces):
        block = env_ref[:, piece * LANES : (piece + 1) * LANES].astype(jnp.float32)
        wide[pl.ds(piece, columns, stride=pieces), :] = block
    rows = columns * pieces
    out_ref[:rows, :] = wide[...].astype(jnp.bfloat16)
    bottom = jnp.concatenate([bottom_ref[...], jnp.zeros((1, LANES - columns), jnp.int32)], axis=1)
    row = lax.broadcasted_iota(jnp.int32, (EXTRA_ROWS, LANES), 0)
    high = lax.shift_right_logical(bottom, 8)
    extra = jnp.where(row == 0, high, jnp.where(row == 1, bottom & (CODE_BASE - 1), 0))
    out_ref[rows:, :] = extra.astype(jnp.float32).astype(jnp.bfloat16)


def propagate(
    track_smem, place_smem, scalars_smem, tracks_ref, starter_ref, prop_ref, own_ref, direct_ref, passed_ref,
    grid_ref, prop, prop_sems, table, bottom_vmem, bottom_smem, bottom_sem,
    field_a, field_b, sin_a, cos_a, sin_b, cos_b, powers,
):
    pieces, double_depth, _ = prop.shape
    depth_cells = double_depth // 2
    steps, bearings = track_smem.shape
    column_total = grid_ref.shape[0]
    block_rows = own_ref.shape[0]
    cell_rows = block_rows - EXTRA_ROWS
    columns_here = cell_rows // pieces
    rounds = direct_ref.shape[0] // block_rows
    per_turn = scalars_smem[0] * jnp.float32(QUARTER_TURN)
    decay = scalars_smem[1]

    loads = [
        pltpu.make_async_copy(
            prop_ref.at[:, piece * LANES : (piece + 1) * LANES], prop.at[piece], prop_sems.at[piece]
        )
        for piece in range(pieces)
    ]
    for load in loads:
        load.start()

    blocks = [own_ref[...]]
    for ref in (direct_ref, passed_ref):
        blocks += [ref[turn * block_rows : (turn + 1) * block_rows, :] for turn in range(rounds)]
    for index, block in enumerate(blocks):
        codes = block[cell_rows:, :].astype(jnp.float32)
        bottom = codes[0:1] * jnp.float32(CODE_BASE) + codes[1:2]
        bottom_vmem[pl.ds(place_smem[index], 1), :] = bottom.astype(jnp.int32)
    to_smem = pltpu.make_async_copy(bottom_vmem, bottom_smem, bottom_sem)
    to_smem.start()
    for index, block in enumerate(blocks):
        rows = pl.ds(pl.multiple_of(place_smem[index] * cell_rows, cell_rows), cell_rows)
        table[rows, :] = block[:cell_rows, :].astype(jnp.float32) * per_turn

    def put(field, cells, real, imaginary):
        beyond = slice(depth_cells + cells.start, depth_cells + cells.stop)
        field[:bearings, cells] = real
        field[:bearings, beyond] = -imaginary
        field[bearings:, cells] = imaginary
        field[bearings:, beyond] = real

    put(field_a, slice(0, depth_cells), starter_ref[:bearings, :], starter_ref[bearings:, :])

    depth_index = lax.broadcasted_iota(jnp.int32, (pieces, LANES), 0) * LANES + lax.broadcasted_iota(
        jnp.int32, (pieces, LANES), 1
    )

    def prepare(step, sin_ref, cos_ref, which):
        for bearing in which:
            column = track_smem[step, bearing]
            owner = lax.div(column, columns_here)
            bottom = bottom_smem[owner, column - owner * columns_here]
            turns = table[pl.ds(pl.multiple_of(column * pieces, pieces), pieces), :]
            sine, cosine, sine_minus, cosine_minus = sine_and_cosine(turns)
            damping = jnp.where(depth_index >= bottom, decay, jnp.float32(1.0))
            rows = slice(bearing * pieces, (bearing + 1) * pieces)
            sin_ref[rows, :] = sine * jnp.where(sine_minus, -damping, damping)
            cos_ref[rows, :] = cosine * jnp.where(cosine_minus, -damping, damping)

    lane = lax.broadcasted_iota(jnp.int32, (bearings, LANES), 1)

    def fold(first, second, width):
        return jnp.where(
            (lane & width) == 0,
            first + pltpu.roll(first, LANES - width, 1),
            second + pltpu.roll(second, width, 1),
        )

    tiles = depth_cells // TILE
    halves = tiles // 2
    pieces_in = 2 * TILE // LANES
    early = [tile + part * tiles for tile in range(tiles - 2) for part in range(2)]
    late = [tile + part * tiles for tile in range(tiles - 2, tiles) for part in range(2)]
    slots_of_step = halves * (len(early) + len(late))
    nothing = jnp.zeros((PAD_ROWS, TILE), jnp.bfloat16)

    def run(*accumulators):
        sums, spare = accumulators[: 2 * halves], accumulators[2 * halves :]
        count = [0]

        def multiply(field, half, tile):
            register = count[0] % 2
            count[0] += 1
            cells = slice(tile * TILE, (tile + 1) * TILE)
            for unit in range(2):
                first = (2 * half + unit) * (TILE // LANES)
                weights = jnp.concatenate([prop[first, cells, :], prop[first + 1, cells, :]], axis=1)
                pltpu.matmul_push_rhs(weights, register, unit)
            for unit in range(2):
                pltpu.matmul_acc_lhs(sums[2 * half + unit], field[:, cells], load_staged_rhs=register)
                pltpu.matmul_acc_lhs(spare[unit], nothing)

        def begin(field):
            for half in range(halves):
                for tile in early:
                    multiply(field, half, tile)

        def advance(step, field, following, sin_ref, cos_ref, next_sin, next_cos):
            work = [[] for _ in range(slots_of_step + 1)]
            share = -(-bearings // slots_of_step)
            coming = jnp.minimum(step + 1, steps - 1)
            for slot in range(slots_of_step):
                which = range(slot * share, min(bearings, (slot + 1) * share))
                work[slot].append(functools.partial(prepare, coming, next_sin, next_cos, which))
            moved = {}
            folded = {}

            def pop(half):
                for unit in range(2):
                    moved[2 * half + unit] = pltpu.matmul_pop(sums[2 * half + unit])

            def screen(piece):
                value = moved[piece * LANES // TILE]
                inner = slice(piece * LANES % TILE, piece * LANES % TILE + LANES)
                moved_re = value[:bearings, inner]
                moved_im = value[bearings:, inner]
                sine = sin_ref[pl.ds(piece, bearings, stride=pieces), :]
                cosine = cos_ref[pl.ds(piece, bearings, stride=pieces), :]
                screened_re = moved_re * cosine - moved_im * sine
                screened_im = moved_re * sine + moved_im * cosine
                outer = slice(piece * LANES, (piece + 1) * LANES)
                put(following, outer, screened_re.astype(jnp.bfloat16), screened_im.astype(jnp.bfloat16))
                level, value = 1, screened_re * screened_re + screened_im * screened_im
                at = piece
                while at % 2 == 1:
                    value = fold(folded.pop((level, at - 1)), value, level)
                    at //= 2
                    level *= 2
                folded[level, at] = value

            for half in range(halves):
                after = (half + 1) * len(late)
                work[after].append(functools.partial(pop, half))
                for index in range(pieces_in):
                    slot = after + 1 + index
                    if half < halves - 1:
                        slot = min(slot, after + len(late) - 1)
                    work[min(slot, slots_of_step)].append(functools.partial(screen, half * pieces_in + index))
            slot = 0
            for source, order in ((field, late), (following, early)):
                for half in range(halves):
                    for tile in order:
                        multiply(source, half, tile)
                        for item in work[slot]:
                            item()
                        slot += 1
            for item in work[slot]:
                item()
            rows = pl.ds(pl.multiple_of(step * bearings, bearings), bearings)
            powers[rows, :] = folded[pieces, 0]

        for load in loads:
            load.wait()
        begin(field_a)
        to_smem.wait()
        prepare(0, sin_a, cos_a, range(bearings))

        def two_steps(pair, carry):
            advance(pair * 2, field_a, field_b, sin_a, cos_a, sin_b, cos_b)
            advance(pair * 2 + 1, field_b, field_a, sin_b, cos_b, sin_a, cos_a)
            return carry

        lax.fori_loop(0, steps // 2, two_steps, 0)
        for accumulator in accumulators:
            pltpu.matmul_pop(accumulator)

    pl.run_scoped(
        run,
        *[pltpu.ACC(unit % 2)((2 * bearings, TILE), jnp.float32) for unit in range(2 * halves)],
        *[pltpu.ACC(unit)((PAD_ROWS, TILE), jnp.float32) for unit in range(2)],
    )

    group = TILE // bearings
    lanes_of_row = lax.broadcasted_iota(jnp.int32, (1, LANES), 1)

    def ids_of(first):
        parts = []
        for start in range(first, first + group, LANES // bearings):
            row = tracks_ref[start : start + 1, :]
            total = jnp.concatenate([row, jnp.zeros((1, LANES - bearings), jnp.int32)], axis=1)
            for index in range(1, LANES // bearings):
                row = tracks_ref[start + index : start + index + 1, :]
                row = jnp.concatenate([row, jnp.zeros((1, LANES - bearings), jnp.int32)], axis=1)
                total = total + pltpu.roll(row, index * bearings, 1)
            parts.append(total)
        return jnp.concatenate(parts, axis=1)

    half_columns = column_total // 2

    def scatter(*sums):
        for index, start in enumerate(range(0, steps, group)):
            ids = ids_of(start)
            value = powers[start * bearings : (start + group) * bearings, :]
            high = value.astype(jnp.bfloat16)
            low = (value - high.astype(jnp.float32)).astype(jnp.bfloat16)
            both = jnp.concatenate([high, low], axis=1)
            for unit in range(2):
                pltpu.matmul_push_rhs(both, index % 2, unit)
            for unit in range(2):
                column = lax.broadcasted_iota(jnp.int32, (half_columns, TILE), 0) + unit * half_columns
                chosen = (column == ids).astype(jnp.bfloat16)
                pltpu.matmul_acc_lhs(sums[unit], chosen, load_staged_rhs=index % 2)
        for unit in range(2):
            total = pltpu.matmul_pop(sums[unit])
            grid_ref[unit * half_columns : (unit + 1) * half_columns, :] = total[:, :LANES] + total[:, LANES:]

    pl.run_scoped(scatter, *[pltpu.ACC(unit)((half_columns, TILE), jnp.float32) for unit in range(2)])


def finish(scale, parts_ref, out_ref):
    total = jnp.sum(parts_ref[...].astype(jnp.float32), axis=0) * jnp.float32(scale)
    row = lax.broadcasted_iota(jnp.int32, (LANES, LANES), 0)
    column = lax.broadcasted_iota(jnp.int32, (LANES, LANES), 1)
    groups = LANES // BAND_CELLS
    place = (row % BAND_CELLS) * groups + row // BAND_CELLS
    order = (place == column).astype(jnp.float32)
    out_ref[...] = jnp.dot(total, order, precision=lax.Precision.HIGHEST, preferred_element_type=jnp.float32)


def on_device(starter, propagator, wavenumber, sediment_loss, env_speed, bottom, track_column):
    bearings_here, steps = track_column.shape
    columns_here, depth_cells = env_speed.shape
    bands = depth_cells // BAND_CELLS
    owners = lax.axis_size("bearing")
    freqs = lax.axis_size("freq")
    devices = owners * freqs
    column_total = columns_here * owners
    pieces = depth_cells // LANES
    smem = pl.BlockSpec(memory_space=pltpu.SMEM)
    vmem = pl.BlockSpec(memory_space=pltpu.VMEM)

    own = pl.pallas_call(
        pack,
        out_shape=jax.ShapeDtypeStruct((columns_here * pieces + EXTRA_ROWS, LANES), jnp.bfloat16),
        in_specs=[vmem] * 2,
        out_specs=vmem,
        scratch_shapes=[pltpu.VMEM((columns_here * pieces, LANES), jnp.float32)],
        name="pack",
    )(env_speed, bottom.reshape(1, -1))

    turns = [(offset, offset - 1) for offset in range(owners - 1, 0, -2)]
    received = []
    for turn in turns:
        pairs = [
            (bearing * freqs + freq, (bearing ^ turn[freq % 2]) * freqs + freq)
            for bearing in range(owners)
            for freq in range(freqs)
            if turn[freq % 2]
        ]
        received.append(lax.ppermute(own, ("bearing", "freq"), pairs))
    direct = jnp.concatenate(received, axis=0)
    passed = lax.ppermute(direct, "freq", [(freq, freq ^ 1) for freq in range(freqs)])

    me = lax.axis_index("bearing")
    core = lax.axis_index("freq") % 2
    offsets = jnp.asarray([[0] + [turn[unit] for unit in order for turn in turns] for order in ((0, 1), (1, 0))], jnp.int32)
    mine = lax.dynamic_index_in_dim(offsets, core, 0, keepdims=False)
    places = jnp.where((mine == 0) & (jnp.arange(mine.shape[0]) > 0), owners, me ^ mine)
    scalars = jnp.stack([wavenumber[0], jnp.exp(-sediment_loss[0])])
    tracks = track_column.T
    grid = pl.pallas_call(
        propagate,
        out_shape=jax.ShapeDtypeStruct((column_total, bands), jnp.float32),
        in_specs=[smem] * 3 + [vmem] * 2 + [pl.BlockSpec(memory_space=pl.ANY)] + [vmem] * 3,
        out_specs=vmem,
        scratch_shapes=[
            pltpu.VMEM((pieces, 2 * depth_cells, LANES), jnp.bfloat16),
            pltpu.SemaphoreType.DMA((pieces,)),
            pltpu.VMEM(((owners + 1) * columns_here * pieces, LANES), jnp.float32),
            pltpu.VMEM((owners + 8, LANES), jnp.int32),
            pltpu.SMEM((owners + 8, LANES), jnp.int32),
            pltpu.SemaphoreType.DMA,
        ]
        + [pltpu.VMEM((2 * bearings_here, 2 * depth_cells), jnp.bfloat16)] * 2
        + [pltpu.VMEM((bearings_here * pieces, LANES), jnp.float32)] * 4
        + [pltpu.VMEM((steps * bearings_here, bands), jnp.float32)],
        compiler_params=pltpu.CompilerParams(vmem_limit_bytes=VMEM_LIMIT),
        name="propagate",
    )(
        tracks, places, scalars, tracks, starter[0].reshape(2 * bearings_here, depth_cells),
        propagator[0].reshape(2 * depth_cells, depth_cells), own, direct, passed,
    )
    parts = lax.all_to_all(
        grid.reshape(devices, column_total // devices, bands), ("bearing", "freq"), 0, 0
    )
    scale = column_total / (bearings_here * owners * steps * freqs)
    return pl.pallas_call(
        functools.partial(finish, scale),
        out_shape=jax.ShapeDtypeStruct((column_total // devices, bands), jnp.float32),
        in_specs=[vmem],
        out_specs=vmem,
        name="finish",
    )(parts)


def solution(mesh):
    in_specs = (
        P("freq", None, "bearing", None),
        P("freq", None, None, None),
        P("freq"),
        P("freq"),
        P("bearing", None),
        P("bearing"),
        P("bearing", None),
    )
    out_specs = P(("bearing", "freq"), None)
    mapped = jax.shard_map(
        on_device, mesh=mesh, in_specs=in_specs, out_specs=out_specs, check_vma=False
    )

    def program(*arrays):
        with jax.sharding.use_abstract_mesh(mesh.abstract_mesh):
            return mapped(*arrays)

    return program
```

time: 81 us -> 59.5 us (0.73)
  blocking collectives: 25.2 us -> 13.3 us
  local copies, waits for them, and re-layouts: 7.52 us -> 0.76 us
  starting transfers between devices: 14.6 us -> 9.97 us
  waiting for transfers between devices: 2.37 us -> 4.09 us
  other arithmetic: 0.08 us -> 1.77 us
  Pallas kernels: 28.8 us -> 27.9 us
    unnamed x1 -> x0, blocking collectives: 11 us -> none
    unnamed x11 -> x7, local copies, waits for them, and re-layouts: 6.74 us -> 0.75 us
    ppermute x7 -> x5, starting transfers between devices: 14.6 us -> 9.97 us  [the longest x4 9.9 us: on_device(): received.append(lax.ppermute(own, ('bearing', 'freq'), pairs))]
    ppermute x7 -> x5, waiting for transfers between devices: 2.37 us -> 4.09 us  [the longest x4 4.09 us: on_device(): received.append(lax.ppermute(own, ('bearing', 'freq'), pairs))]
    select_n x0 -> x1, other arithmetic: none -> 1.2 us  [on_device(): jnp.where((mine == 0) & (jnp.arange(mine.shape[0]) > 0), owners, me ^ mine)]
    pallas_call x1 -> x2, Pallas kernels: 27.1 us -> 26.2 us  [the longest x1 24.7 us: on_device(): pl.pallas_call(propagate, out_shape=jax.ShapeDtypeStruct((column_total, b...]
    all_to_all x1, blocking collectives: 14.2 us -> 13.3 us  [on_device(): lax.all_to_all(grid.reshape(devices, column_total // devices, bands), ('b...]
  transfers between devices with their start and end apart: 7 -> 5, of which waited for: 1 -> 2; matrix products, arithmetic and copies ran while one was open for 4% -> 3% of each run, Pallas kernels for 0% -> 0%
where the time goes in v2:
time: 59.5 us; the launch traced here: 59.2 us
  Pallas kernels  27.9 us (47%)
  blocking collectives  13.3 us (22%)
  starting transfers between devices  9.97 us (17%)
  waiting for transfers between devices  4.09 us (7%)
  other arithmetic  1.77 us (3%)
  between operations  1.44 us (2%)
  local copies, waits for them, and re-layouts  0.76 us (1%)
    pallas_call x1, Pallas kernels, on_device(): pl.pallas_call(propagate, out_shape=jax.ShapeDtypeStruct((column_total, b...  24.7 us
    all_to_all x1, blocking collectives, on_device(): lax.all_to_all(grid.reshape(devices, column_total // devices, bands), ('b...  13.3 us
    ppermute x4, starting transfers between devices, on_device(): received.append(lax.ppermute(own, ('bearing', 'freq'), pairs))  9.9 us
    ppermute x4, waiting for transfers between devices, on_device(): received.append(lax.ppermute(own, ('bearing', 'freq'), pairs))  4.09 us
    pallas_call x1, Pallas kernels, on_device(): pl.pallas_call(functools.partial(finish, scale), out_shape=jax.ShapeDtype...  1.7 us
    pallas_call x1, Pallas kernels, on_device(): pl.pallas_call(pack, out_shape=jax.ShapeDtypeStruct((columns_here * piece...  1.5 us
    select_n x1, other arithmetic, on_device(): jnp.where((mine == 0) & (jnp.arange(mine.shape[0]) > 0), owners, me ^ mine)  1.2 us
  transfers between devices with their start and end apart: 5, of which 2 were waited for; matrix products, arithmetic and copies ran while one was open for 3% of the time, Pallas kernels for 0%

profile of v2, /device:TPU:0, one launch (start us, length us, event | category | flops | bytes accessed | tf_op | source)
XLA Modules:
  0.0 59.2 jit_solution(313974308784422865)
XLA Ops:
  0.0 1.5 %pack.1.own_ref = bf16[272,128]{1,0:T(8,128)(2,1)} custom-call(bf16[32,1024]{1,0:T(8,128)(2,1)} %env_ref.1, s32[1,32]{1,0:T(1,128)} %bitcast.16), custom_call_target="tpu_custom_call" | custom-call | tf_op jit(solution)/shard_map/pack/pallas_call | solution.py:295
  1.5 6.0 %collective-permute-start = (bf16[272,128]{1,0:T(8,128)(2,1)}, bf16[272,128]{1,0:T(8,128)(2,1)S(1)}, u32[]{:S(2)}, u32[]{:S(2)}) collective-permute-start(bf16[272,128]{1,0:T(8,128)(2,1)} %pack.1.own_ref), channel_id=1, source_target_pairs={{0,28},{1,25},{2,30},{3,27},{4,24},{5,29},{6,26},{7,31},{8,20},{9,... | collective-permute-start | bytes 208904 | tf_op jit(solution)/shard_map/ppermute | solution.py:313
  7.5 0.0 collective-permute-start.1
  7.5 1.7 %collective-permute-start.2 = (bf16[272,128]{1,0:T(8,128)(2,1)}, bf16[272,128]{1,0:T(8,128)(2,1)S(1)}, u32[]{:S(2)}, u32[]{:S(2)}) collective-permute-start(bf16[272,128]{1,0:T(8,128)(2,1)} %pack.1.own_ref), channel_id=1, source_target_pairs={{0,12},{1,9},{2,14},{3,11},{4,8},{5,13},{6,10},{7,15},{8,4},{9,1},... | collective-permute-start | bytes 208904 | tf_op jit(solution)/shard_map/ppermute | solution.py:313
  9.2 2.2 %collective-permute-start.3 = (bf16[272,128]{1,0:T(8,128)(2,1)}, bf16[272,128]{1,0:T(8,128)(2,1)S(1)}, u32[]{:S(2)}, u32[]{:S(2)}) collective-permute-start(bf16[272,128]{1,0:T(8,128)(2,1)} %pack.1.own_ref), channel_id=1, source_target_pairs={{0,4},{2,6},{4,0},{6,2},{8,12},{10,14},{12,8},{14,10},{16,20},{18,... | collective-permute-start | bytes 208904 | tf_op jit(solution)/shard_map/ppermute | solution.py:313
  11.4 0.0 collective-permute-done
  11.4 2.6 %collective-permute-done.1 = bf16[272,128]{1,0:T(8,128)(2,1)S(1)} collective-permute-done((bf16[272,128]{1,0:T(8,128)(2,1)}, bf16[272,128]{1,0:T(8,128)(2,1)S(1)}, u32[]{:S(2)}, u32[]{:S(2)}) %collective-permute-start.1) | collective-permute-done | bytes 69664 | tf_op jit(solution)/shard_map/ppermute | solution.py:313
  14.1 0.0 collective-permute-done.2
  14.1 1.5 %collective-permute-done.3 = bf16[272,128]{1,0:T(8,128)(2,1)S(1)} collective-permute-done((bf16[272,128]{1,0:T(8,128)(2,1)}, bf16[272,128]{1,0:T(8,128)(2,1)S(1)}, u32[]{:S(2)}, u32[]{:S(2)}) %collective-permute-start.3) | collective-permute-done | bytes 69664 | tf_op jit(solution)/shard_map/ppermute | solution.py:313
  15.6 0.0 copy-start
  15.6 0.1 collective-permute-start.4
  17.0 0.6 pad_maximum_fusion.scalars_smem
  17.6 1.2 %fusion.place_smem = s32[9]{0:T(128)} fusion(s32[2,9]{1,0:T(2,128)} %constant.31.clone, s32[]{:T(128)S(6)} %select_n.16, s32[]{:T(128)S(6)} %axis_index.25), kind=kLoop, calls=%fused_computation.5 | loop fusion | flops 45 | bytes 80 | tf_op jit(solution)/shard_map/jit(_where)/select_n | solution.py:321
  18.8 0.0 collective-permute-done.4.passed_ref
  18.8 0.0 copy-start.1
  18.8 0.0 copy-done
  18.8 0.7 %copy-done.1 = bf16[1088,128]{1,0:T(8,128)(2,1)} copy-done((bf16[1088,128]{1,0:T(8,128)(2,1)}, bf16[1088,128]{1,0:T(8,128)(2,1)S(1)}, u32[]{:S(2)}) %copy-start.1) | copy-done | bytes 278552
  19.5 24.7 %propagate.1 = f32[256,128]{1,0:T(8,128)} custom-call(s32[24,32]{1,0:T(8,128)} %bitcast.14, s32[9]{0:T(128)} %fusion.place_smem, f32[2]{0:T(128)} %pad_maximum_fusion.scalars_smem, s32[24,32]{1,0:T(8,128)} %bitcast.15, bf16[64,1024]{1,0:T(8,128)(2,1)} %bitcast.13, bf16[2048,1024]{1,0:T(8,128)(2,1)} %bitcast.11, bf16[272,128]{1,0:T(8,128)(2,1)} %pack.1.own_ref, ...), custom_call_target="tpu_custom_call" | custom-call | tf_op jit(solution)/shard_map/propagate/pallas_call | solution.py:324
  44.2 13.3 %all_to_all.5.parts_ref = f32[32,8,128]{2,1,0:T(8,128)} all-to-all(f32[32,8,128]{2,1,0:T(8,128)} %bitcast.12), channel_id=1, replica_groups=mesh['bearing'=8,'freq'=4] {'bearing','freq'}, dimensions={0} | all-to-all | bytes 262144 | tf_op jit(solution)/shard_map/all_to_all | solution.py:346
  57.5 1.7 %finish.1 = f32[8,128]{1,0:T(8,128)} custom-call(f32[32,8,128]{2,1,0:T(8,128)} %all_to_all.5.parts_ref), custom_call_target="tpu_custom_call" | custom-call | tf_op jit(solution)/shard_map/finish/pallas_call | solution.py:350
  (4 shorter events, 0.0 us)
Async XLA Ops:
  1.5 9.9 %collective-permute-start = (bf16[272,128]{1,0:T(8,128)(2,1)}, bf16[272,128]{1,0:T(8,128)(2,1)S(1)}, u32[]{:S(2)}, u32[]{:S(2)}) collective-permute-start(bf16[272,128]{1,0:T(8,128)(2,1)} %pack.1.own_ref), channel_id=1, source_target_pairs={{0,28},{1,25},{2,30},{3,27},{4,24},{5,29},{6,26},{7,31},{8,20},{9,... | collective-permute-start | bytes 208904 | tf_op jit(solution)/shard_map/ppermute | solution.py:313
  7.5 6.6 %collective-permute-start.1 = (bf16[272,128]{1,0:T(8,128)(2,1)}, bf16[272,128]{1,0:T(8,128)(2,1)S(1)}, u32[]{:S(2)}, u32[]{:S(2)}) collective-permute-start(bf16[272,128]{1,0:T(8,128)(2,1)} %pack.1.own_ref), channel_id=1, source_target_pairs={{0,20},{1,17},{2,22},{3,19},{4,16},{5,21},{6,18},{7,23},{8,28},{9,... | collective-permute-start | bytes 208904 | tf_op jit(solution)/shard_map/ppermute | solution.py:313
  7.5 6.6 %collective-permute-start.2 = (bf16[272,128]{1,0:T(8,128)(2,1)}, bf16[272,128]{1,0:T(8,128)(2,1)S(1)}, u32[]{:S(2)}, u32[]{:S(2)}) collective-permute-start(bf16[272,128]{1,0:T(8,128)(2,1)} %pack.1.own_ref), channel_id=1, source_target_pairs={{0,12},{1,9},{2,14},{3,11},{4,8},{5,13},{6,10},{7,15},{8,4},{9,1},... | collective-permute-start | bytes 208904 | tf_op jit(solution)/shard_map/ppermute | solution.py:313
  9.2 6.4 %collective-permute-start.3 = (bf16[272,128]{1,0:T(8,128)(2,1)}, bf16[272,128]{1,0:T(8,128)(2,1)S(1)}, u32[]{:S(2)}, u32[]{:S(2)}) collective-permute-start(bf16[272,128]{1,0:T(8,128)(2,1)} %pack.1.own_ref), channel_id=1, source_target_pairs={{0,4},{2,6},{4,0},{6,2},{8,12},{10,14},{12,8},{14,10},{16,20},{18,... | collective-permute-start | bytes 208904 | tf_op jit(solution)/shard_map/ppermute | solution.py:313
  15.6 3.2 %copy-start = (bf16[1088,128]{1,0:T(8,128)(2,1)}, bf16[1088,128]{1,0:T(8,128)(2,1)S(1)}, u32[]{:S(2)}) copy-start(bf16[1088,128]{1,0:T(8,128)(2,1)S(1)} %constant_dynamic-update-slice_fusion.direct_ref) | copy-start | bytes 835588
  15.6 3.2 %collective-permute-start.4 = (bf16[1088,128]{1,0:T(8,128)(2,1)S(1)}, bf16[1088,128]{1,0:T(8,128)(2,1)S(1)}, u32[]{:S(2)}, u32[]{:S(2)}) collective-permute-start(bf16[1088,128]{1,0:T(8,128)(2,1)S(1)} %constant_dynamic-update-slice_fusion.direct_ref), channel_id=1, source_target_pairs={{0,1},{1,0},{2,3},{3,2},{4,5},{5,4},{6,7},{7,6},{8,9},{9,8},{10,11... | collective-permute-start | bytes 835592 | tf_op jit(solution)/shard_map/ppermute | solution.py:315
  18.8 0.7 %copy-start.1 = (bf16[1088,128]{1,0:T(8,128)(2,1)}, bf16[1088,128]{1,0:T(8,128)(2,1)S(1)}, u32[]{:S(2)}) copy-start(bf16[1088,128]{1,0:T(8,128)(2,1)S(1)} %collective-permute-done.4.passed_ref) | copy-start | bytes 835588

commit v3 on v2

--- a/solution.py
+++ b/solution.py
@@ -16,7 +16,8 @@
 QUARTER_TURN = 0.6366197723675814
 SIN_TERMS = (1.5707963219600276, -0.6459634781534198, 0.079680222858126, -0.004602163104811149)
 COS_TERMS = (0.9999999723759501, -1.2336970108360321, 0.25359860771245774, -0.020408255467132635)
-VMEM_LIMIT = 60 * 1024 * 1024
+VMEM_LIMIT = 24 * 1024 * 1024
+SPREAD_LIMIT = 24 * 1024 * 1024
 
 
 def polynomial(terms, square):
@@ -57,9 +58,22 @@
     out_ref[rows:, :] = extra.astype(jnp.float32).astype(jnp.bfloat16)
 
 
+def spread(prop_ref, out_ref, sems):
+    loads = [
+        pltpu.make_async_copy(
+            prop_ref.at[:, piece * LANES : (piece + 1) * LANES], out_ref.at[piece], sems.at[piece]
+        )
+        for piece in range(out_ref.shape[0])
+    ]
+    for load in loads:
+        load.start()
+    for load in loads:
+        load.wait()
+
+
 def propagate(
-    track_smem, place_smem, scalars_smem, tracks_ref, starter_ref, prop_ref, own_ref, direct_ref, passed_ref,
-    grid_ref, prop, prop_sems, table, bottom_vmem, bottom_smem, bottom_sem,
+    track_smem, wavenumber_smem, loss_smem, tracks_ref, starter_ref, prop, own_ref, direct_ref, passed_ref,
+    grid_ref, sin_table, cos_table,
     field_a, field_b, sin_a, cos_a, sin_b, cos_b, powers,
 ):
     pieces, double_depth, _ = prop.shape
@@ -70,30 +84,47 @@
     cell_rows = block_rows - EXTRA_ROWS
     columns_here = cell_rows // pieces
     rounds = direct_ref.shape[0] // block_rows
-    per_turn = scalars_smem[0] * jnp.float32(QUARTER_TURN)
-    decay = scalars_smem[1]
-
-    loads = [
-        pltpu.make_async_copy(
-            prop_ref.at[:, piece * LANES : (piece + 1) * LANES], prop.at[piece], prop_sems.at[piece]
-        )
-        for piece in range(pieces)
-    ]
-    for load in loads:
-        load.start()
-
-    blocks = [own_ref[...]]
-    for ref in (direct_ref, passed_ref):
-        blocks += [ref[turn * block_rows : (turn + 1) * block_rows, :] for turn in range(rounds)]
-    for index, block in enumerate(blocks):
-        codes = block[cell_rows:, :].astype(jnp.float32)
-        bottom = codes[0:1] * jnp.float32(CODE_BASE) + codes[1:2]
-        bottom_vmem[pl.ds(place_smem[index], 1), :] = bottom.astype(jnp.int32)
-    to_smem = pltpu.make_async_copy(bottom_vmem, bottom_smem, bottom_sem)
-    to_smem.start()
-    for index, block in enumerate(blocks):
-        rows = pl.ds(pl.multiple_of(place_smem[index] * cell_rows, cell_rows), cell_rows)
-        table[rows, :] = block[:cell_rows, :].astype(jnp.float32) * per_turn
+    stride = pieces + 1
+    per_turn = wavenumber_smem[0] * jnp.float32(QUARTER_TURN)
+    decay = jnp.exp(jnp.full((pieces, LANES), -loss_smem[0], jnp.float32))
+    me = lax.axis_index("bearing")
+    core = lax.axis_index("freq") % 2
+    owners = 2 * rounds
+
+    def place_of(turn, unit):
+        offset = owners - 1 - 2 * turn - unit
+        return jnp.where(offset == 0, owners, me ^ offset)
+
+    depth_index = lax.broadcasted_iota(jnp.int32, (pieces, LANES), 0) * LANES + lax.broadcasted_iota(
+        jnp.int32, (pieces, LANES), 1
+    )
+    depth_index = depth_index.astype(jnp.float32)
+
+    def tabulate(ref, place, start):
+        base = place * cell_rows
+        codes = ref[pl.ds(start + cell_rows, EXTRA_ROWS), :].astype(jnp.float32)
+        bottoms = codes[0:1] * jnp.float32(CODE_BASE) + codes[1:2]
+        bottoms = jnp.broadcast_to(bottoms, (pieces, LANES))
+        for pair in range(columns_here // 2):
+            both = ref[pl.ds(pl.multiple_of(start + pair * 2 * pieces, 2 * pieces), 2 * pieces), :]
+            both = both.astype(jnp.float32) * per_turn
+            for column in (2 * pair, 2 * pair + 1):
+                inner = (column - 2 * pair) * pieces
+                sine, cosine, sine_minus, cosine_minus = sine_and_cosine(both[inner : inner + pieces])
+                bottom = jnp.broadcast_to(bottoms[:, column : column + 1], (pieces, LANES))
+                damping = jnp.where(depth_index >= bottom, decay, jnp.float32(1.0))
+                rows = pl.ds(pl.multiple_of(base + column * pieces, pieces), pieces)
+                sin_table[rows, :] = sine * jnp.where(sine_minus, -damping, damping)
+                cos_table[rows, :] = cosine * jnp.where(cosine_minus, -damping, damping)
+
+    tabulate(own_ref, me, 0)
+    for index, ref in enumerate((direct_ref, passed_ref)):
+
+        def one(turn, carry, ref=ref, index=index):
+            tabulate(ref, place_of(turn, core ^ index), turn * block_rows)
+            return carry
+
+        lax.fori_loop(0, rounds, one, 0)
 
     def put(field, cells, real, imaginary):
         beyond = slice(depth_cells + cells.start, depth_cells + cells.stop)
@@ -104,21 +135,12 @@
 
     put(field_a, slice(0, depth_cells), starter_ref[:bearings, :], starter_ref[bearings:, :])
 
-    depth_index = lax.broadcasted_iota(jnp.int32, (pieces, LANES), 0) * LANES + lax.broadcasted_iota(
-        jnp.int32, (pieces, LANES), 1
-    )
-
     def prepare(step, sin_ref, cos_ref, which):
         for bearing in which:
             column = track_smem[step, bearing]
-            owner = lax.div(column, columns_here)
-            bottom = bottom_smem[owner, column - owner * columns_here]
-            turns = table[pl.ds(pl.multiple_of(column * pieces, pieces), pieces), :]
-            sine, cosine, sine_minus, cosine_minus = sine_and_cosine(turns)
-            damping = jnp.where(depth_index >= bottom, decay, jnp.float32(1.0))
-            rows = slice(bearing * pieces, (bearing + 1) * pieces)
-            sin_ref[rows, :] = sine * jnp.where(sine_minus, -damping, damping)
-            cos_ref[rows, :] = cosine * jnp.where(cosine_minus, -damping, damping)
+            rows = pl.ds(pl.multiple_of(column * pieces, pieces), pieces)
+            sin_ref[bearing * stride : bearing * stride + pieces, :] = sin_table[rows, :]
+            cos_ref[bearing * stride : bearing * stride + pieces, :] = cos_table[rows, :]
 
     lane = lax.broadcasted_iota(jnp.int32, (bearings, LANES), 1)
 
@@ -177,8 +199,8 @@
                 inner = slice(piece * LANES % TILE, piece * LANES % TILE + LANES)
                 moved_re = value[:bearings, inner]
                 moved_im = value[bearings:, inner]
-                sine = sin_ref[pl.ds(piece, bearings, stride=pieces), :]
-                cosine = cos_ref[pl.ds(piece, bearings, stride=pieces), :]
+                sine = sin_ref[pl.ds(piece, bearings, stride=stride), :]
+                cosine = cos_ref[pl.ds(piece, bearings, stride=stride), :]
                 screened_re = moved_re * cosine - moved_im * sine
                 screened_im = moved_re * sine + moved_im * cosine
                 outer = slice(piece * LANES, (piece + 1) * LANES)
@@ -212,18 +234,18 @@
             rows = pl.ds(pl.multiple_of(step * bearings, bearings), bearings)
             powers[rows, :] = folded[pieces, 0]
 
-        for load in loads:
-            load.wait()
         begin(field_a)
-        to_smem.wait()
         prepare(0, sin_a, cos_a, range(bearings))
 
-        def two_steps(pair, carry):
-            advance(pair * 2, field_a, field_b, sin_a, cos_a, sin_b, cos_b)
-            advance(pair * 2 + 1, field_b, field_a, sin_b, cos_b, sin_a, cos_a)
+        together = 4 if steps % 4 == 0 else 2
+
+        def some_steps(index, carry):
+            for step in range(0, together, 2):
+                advance(index * together + step, field_a, field_b, sin_a, cos_a, sin_b, cos_b)
+                advance(index * together + step + 1, field_b, field_a, sin_b, cos_b, sin_a, cos_a)
             return carry
 
-        lax.fori_loop(0, steps // 2, two_steps, 0)
+        lax.fori_loop(0, steps // together, some_steps, 0)
         for accumulator in accumulators:
             pltpu.matmul_pop(accumulator)
 
@@ -276,8 +298,16 @@
     column = lax.broadcasted_iota(jnp.int32, (LANES, LANES), 1)
     groups = LANES // BAND_CELLS
     place = (row % BAND_CELLS) * groups + row // BAND_CELLS
-    order = (place == column).astype(jnp.float32)
-    out_ref[...] = jnp.dot(total, order, precision=lax.Precision.HIGHEST, preferred_element_type=jnp.float32)
+    order = (place == column).astype(jnp.bfloat16)
+    rows = total.shape[0]
+    parts = []
+    for _ in range(3):
+        part = total.astype(jnp.bfloat16)
+        total = total - part.astype(jnp.float32)
+        parts.append(part.astype(jnp.float32))
+    parts = jnp.concatenate(parts, axis=0).astype(jnp.bfloat16)
+    placed = jnp.dot(parts, order, preferred_element_type=jnp.float32)
+    out_ref[...] = placed[:rows] + (placed[rows : 2 * rows] + placed[2 * rows :])
 
 
 def on_device(starter, propagator, wavenumber, sediment_loss, env_speed, bottom, track_column):
@@ -311,37 +341,38 @@
             if turn[freq % 2]
         ]
         received.append(lax.ppermute(own, ("bearing", "freq"), pairs))
+    spread_out = pl.pallas_call(
+        spread,
+        out_shape=jax.ShapeDtypeStruct((pieces, 2 * depth_cells, LANES), jnp.bfloat16),
+        in_specs=[pl.BlockSpec(memory_space=pl.ANY)],
+        out_specs=vmem,
+        scratch_shapes=[pltpu.SemaphoreType.DMA((pieces,))],
+        compiler_params=pltpu.CompilerParams(vmem_limit_bytes=SPREAD_LIMIT),
+        cost_estimate=pl.CostEstimate(flops=0, bytes_accessed=2 * propagator.size * 2, transcendentals=0),
+        name="spread",
+    )(propagator[0].reshape(2 * depth_cells, depth_cells))
     direct = jnp.concatenate(received, axis=0)
+    direct, spread_out = lax.optimization_barrier((direct, spread_out))
     passed = lax.ppermute(direct, "freq", [(freq, freq ^ 1) for freq in range(freqs)])
 
-    me = lax.axis_index("bearing")
-    core = lax.axis_index("freq") % 2
-    offsets = jnp.asarray([[0] + [turn[unit] for unit in order for turn in turns] for order in ((0, 1), (1, 0))], jnp.int32)
-    mine = lax.dynamic_index_in_dim(offsets, core, 0, keepdims=False)
-    places = jnp.where((mine == 0) & (jnp.arange(mine.shape[0]) > 0), owners, me ^ mine)
-    scalars = jnp.stack([wavenumber[0], jnp.exp(-sediment_loss[0])])
     tracks = track_column.T
     grid = pl.pallas_call(
         propagate,
         out_shape=jax.ShapeDtypeStruct((column_total, bands), jnp.float32),
-        in_specs=[smem] * 3 + [vmem] * 2 + [pl.BlockSpec(memory_space=pl.ANY)] + [vmem] * 3,
+        in_specs=[smem] * 3 + [vmem] * 6,
         out_specs=vmem,
         scratch_shapes=[
-            pltpu.VMEM((pieces, 2 * depth_cells, LANES), jnp.bfloat16),
-            pltpu.SemaphoreType.DMA((pieces,)),
             pltpu.VMEM(((owners + 1) * columns_here * pieces, LANES), jnp.float32),
-            pltpu.VMEM((owners + 8, LANES), jnp.int32),
-            pltpu.SMEM((owners + 8, LANES), jnp.int32),
-            pltpu.SemaphoreType.DMA,
+            pltpu.VMEM(((owners + 1) * columns_here * pieces, LANES), jnp.float32),
         ]
         + [pltpu.VMEM((2 * bearings_here, 2 * depth_cells), jnp.bfloat16)] * 2
-        + [pltpu.VMEM((bearings_here * pieces, LANES), jnp.float32)] * 4
+        + [pltpu.VMEM((bearings_here * (pieces + 1), LANES), jnp.float32)] * 4
         + [pltpu.VMEM((steps * bearings_here, bands), jnp.float32)],
         compiler_params=pltpu.CompilerParams(vmem_limit_bytes=VMEM_LIMIT),
         name="propagate",
     )(
-        tracks, places, scalars, tracks, starter[0].reshape(2 * bearings_here, depth_cells),
-        propagator[0].reshape(2 * depth_cells, depth_cells), own, direct, passed,
+        tracks, wavenumber, sediment_loss, tracks, starter[0].reshape(2 * bearings_here, depth_cells),
+        spread_out, own, direct, passed,
     )
     parts = lax.all_to_all(
         grid.reshape(devices, column_total // devices, bands), ("bearing", "freq"), 0, 0

time: 59.5 us -> 51.8 us (0.87)
  Pallas kernels: 27.9 us -> 23.2 us
  blocking collectives: 13.3 us -> 10.6 us
  other arithmetic: 1.77 us -> 0.02 us
  local copies, waits for them, and re-layouts: 0.76 us -> 2.2 us
    pallas_call x1, Pallas kernels: 24.7 us -> 18.8 us  [on_device(): pl.pallas_call(propagate, out_shape=jax.ShapeDtypeStruct((column_total, b...]
    all_to_all x1, blocking collectives: 13.3 us -> 10.6 us  [on_device(): lax.all_to_all(grid.reshape(devices, column_total // devices, bands), ('b...]
    unnamed x7 -> x8, local copies, waits for them, and re-layouts: 0.75 us -> 2.2 us
    select_n x1 -> x0, other arithmetic: 1.2 us -> none  [on_device(): jnp.where((mine == 0) & (jnp.arange(mine.shape[0]) > 0), owners, me ^ mine)]
    pallas_call x0 -> x1, Pallas kernels: none -> 1.17 us  [on_device(): pl.pallas_call(spread, out_shape=jax.ShapeDtypeStruct((pieces, 2 * depth_...]
  transfers between devices with their start and end apart: 5 -> 5, of which waited for: 2 -> 3; matrix products, arithmetic and copies ran while one was open for 3% -> 0% of each run, Pallas kernels for 0% -> 2%
where the time goes in v3:
time: 51.8 us; the launch traced here: 51.5 us
  Pallas kernels  23.2 us (45%)
  blocking collectives  10.6 us (20%)
  starting transfers between devices  10 us (19%)
  waiting for transfers between devices  4.08 us (8%)
  local copies, waits for them, and re-layouts  2.2 us (4%)
  between operations  1.36 us (3%)
    pallas_call x1, Pallas kernels, on_device(): pl.pallas_call(propagate, out_shape=jax.ShapeDtypeStruct((column_total, b...  18.8 us
    all_to_all x1, blocking collectives, on_device(): lax.all_to_all(grid.reshape(devices, column_total // devices, bands), ('b...  10.6 us
    ppermute x4, starting transfers between devices, on_device(): received.append(lax.ppermute(own, ('bearing', 'freq'), pairs))  9.97 us
    ppermute x4, waiting for transfers between devices, on_device(): received.append(lax.ppermute(own, ('bearing', 'freq'), pairs))  3.83 us
    unnamed x8, local copies, waits for them, and re-layouts  2.2 us
    pallas_call x1, Pallas kernels, on_device(): pl.pallas_call(functools.partial(finish, scale), out_shape=jax.ShapeDtype...  1.67 us
    pallas_call x1, Pallas kernels, on_device(): pl.pallas_call(pack, out_shape=jax.ShapeDtypeStruct((columns_here * piece...  1.5 us
    pallas_call x1, Pallas kernels, on_device(): pl.pallas_call(spread, out_shape=jax.ShapeDtypeStruct((pieces, 2 * depth_...  1.17 us
  transfers between devices with their start and end apart: 5, of which 3 were waited for; matrix products, arithmetic and copies ran while one was open for 0% of the time, Pallas kernels for 2%

profile of v3, /device:TPU:0, one launch (start us, length us, event | category | flops | bytes accessed | tf_op | source)
XLA Modules:
  0.0 51.5 jit_solution(6787307942521193238)
XLA Ops:
  0.0 1.5 %pack.1.own_ref = bf16[272,128]{1,0:T(8,128)(2,1)} custom-call(bf16[32,1024]{1,0:T(8,128)(2,1)} %env_ref.1, s32[1,32]{1,0:T(1,128)} %bitcast.10), custom_call_target="tpu_custom_call" | custom-call | tf_op jit(solution)/shard_map/pack/pallas_call | solution.py:325
  1.5 4.8 %collective-permute-start.3 = (bf16[272,128]{1,0:T(8,128)(2,1)}, bf16[272,128]{1,0:T(8,128)(2,1)S(1)}, u32[]{:S(2)}, u32[]{:S(2)}) collective-permute-start(bf16[272,128]{1,0:T(8,128)(2,1)} %pack.1.own_ref), channel_id=1, source_target_pairs={{0,4},{2,6},{4,0},{6,2},{8,12},{10,14},{12,8},{14,10},{16,20},{18,... | collective-permute-start | bytes 208904 | tf_op jit(solution)/shard_map/ppermute | solution.py:343
  6.3 1.6 %collective-permute-start.2 = (bf16[272,128]{1,0:T(8,128)(2,1)}, bf16[272,128]{1,0:T(8,128)(2,1)S(1)}, u32[]{:S(2)}, u32[]{:S(2)}) collective-permute-start(bf16[272,128]{1,0:T(8,128)(2,1)} %pack.1.own_ref), channel_id=1, source_target_pairs={{0,12},{1,9},{2,14},{3,11},{4,8},{5,13},{6,10},{7,15},{8,4},{9,1},... | collective-permute-start | bytes 208904 | tf_op jit(solution)/shard_map/ppermute | solution.py:343
  8.0 3.5 %collective-permute-start.1 = (bf16[272,128]{1,0:T(8,128)(2,1)}, bf16[272,128]{1,0:T(8,128)(2,1)S(1)}, u32[]{:S(2)}, u32[]{:S(2)}) collective-permute-start(bf16[272,128]{1,0:T(8,128)(2,1)} %pack.1.own_ref), channel_id=1, source_target_pairs={{0,20},{1,17},{2,22},{3,19},{4,16},{5,21},{6,18},{7,23},{8,28},{9,... | collective-permute-start | bytes 208904 | tf_op jit(solution)/shard_map/ppermute | solution.py:343
  11.5 0.0 collective-permute-start
  11.5 0.0 copy-start
  11.5 2.2 %copy-done = bf16[1,2,1024,1024]{3,2,1,0:T(8,128)(2,1)S(1)} copy-done((bf16[1,2,1024,1024]{3,2,1,0:T(8,128)(2,1)S(1)}, bf16[1,2,1024,1024]{3,2,1,0:T(8,128)(2,1)}, u32[]{:S(2)}) %copy-start) | copy-done | bytes 4194328
  13.7 0.0 copy-start.1
  13.7 0.0 copy-start.2
  13.7 0.0 copy-start.3
  13.7 1.2 %spread.1.prop = bf16[8,2048,128]{2,1,0:T(8,128)(2,1)S(1)} custom-call(bf16[2048,1024]{1,0:T(8,128)(2,1)S(1)} %bitcast.5), custom_call_target="tpu_custom_call" | custom-call | bytes 8388608 | tf_op jit(solution)/shard_map/spread/pallas_call | solution.py:344
  14.9 0.0 collective-permute-done.3
  14.9 0.0 collective-permute-done.2
  14.9 0.3 collective-permute-done.1
  15.1 3.6 %collective-permute-done = bf16[272,128]{1,0:T(8,128)(2,1)S(1)} collective-permute-done((bf16[272,128]{1,0:T(8,128)(2,1)}, bf16[272,128]{1,0:T(8,128)(2,1)S(1)}, u32[]{:S(2)}, u32[]{:S(2)}) %collective-permute-start) | collective-permute-done | bytes 69664 | tf_op jit(solution)/shard_map/ppermute | solution.py:343
  18.7 0.1 collective-permute-start.4
  20.1 0.3 collective-permute-done.4.passed_ref
  20.3 0.0 copy-done.1
  20.3 0.0 copy-done.2
  20.3 0.0 copy-done.3
  20.4 18.8 %propagate.1 = f32[256,128]{1,0:T(8,128)S(1)} custom-call(s32[24,32]{1,0:T(8,128)S(1)} %bitcast.8, f32[1]{0:T(128)S(6)} %copy.8.wavenumber_smem, f32[1]{0:T(128)S(6)} %copy.9.loss_smem, s32[24,32]{1,0:T(8,128)S(1)} %bitcast.9, bf16[64,1024]{1,0:T(8,128)(2,1)S(1)} %bitcast.7, bf16[8,2048,128]{2,1,0:T(8,128)(2,1)S(1)} %spread.1.prop, ...), custom_call_target="tpu_custom_call" | custom-call | tf_op jit(solution)/shard_map/propagate/pallas_call | solution.py:359
  39.2 10.6 %all_to_all.5.parts_ref = f32[32,8,128]{2,1,0:T(8,128)} all-to-all(f32[32,8,128]{2,1,0:T(8,128)S(1)} %bitcast.6), channel_id=1, replica_groups=mesh['bearing'=8,'freq'=4] {'bearing','freq'}, dimensions={0} | all-to-all | bytes 262144 | tf_op jit(solution)/shard_map/all_to_all | solution.py:377
  49.8 1.7 %finish.1 = f32[8,128]{1,0:T(8,128)} custom-call(f32[32,8,128]{2,1,0:T(8,128)} %all_to_all.5.parts_ref), custom_call_target="tpu_custom_call" | custom-call | tf_op jit(solution)/shard_map/finish/pallas_call | solution.py:381
  (1 shorter events, 0.0 us)
Async XLA Ops:
  1.5 13.3 %collective-permute-start.3 = (bf16[272,128]{1,0:T(8,128)(2,1)}, bf16[272,128]{1,0:T(8,128)(2,1)S(1)}, u32[]{:S(2)}, u32[]{:S(2)}) collective-permute-start(bf16[272,128]{1,0:T(8,128)(2,1)} %pack.1.own_ref), channel_id=1, source_target_pairs={{0,4},{2,6},{4,0},{6,2},{8,12},{10,14},{12,8},{14,10},{16,20},{18,... | collective-permute-start | bytes 208904 | tf_op jit(solution)/shard_map/ppermute | solution.py:343
  6.3 8.5 %collective-permute-start.2 = (bf16[272,128]{1,0:T(8,128)(2,1)}, bf16[272,128]{1,0:T(8,128)(2,1)S(1)}, u32[]{:S(2)}, u32[]{:S(2)}) collective-permute-start(bf16[272,128]{1,0:T(8,128)(2,1)} %pack.1.own_ref), channel_id=1, source_target_pairs={{0,12},{1,9},{2,14},{3,11},{4,8},{5,13},{6,10},{7,15},{8,4},{9,1},... | collective-permute-start | bytes 208904 | tf_op jit(solution)/shard_map/ppermute | solution.py:343
  8.0 7.2 %collective-permute-start.1 = (bf16[272,128]{1,0:T(8,128)(2,1)}, bf16[272,128]{1,0:T(8,128)(2,1)S(1)}, u32[]{:S(2)}, u32[]{:S(2)}) collective-permute-start(bf16[272,128]{1,0:T(8,128)(2,1)} %pack.1.own_ref), channel_id=1, source_target_pairs={{0,20},{1,17},{2,22},{3,19},{4,16},{5,21},{6,18},{7,23},{8,28},{9,... | collective-permute-start | bytes 208904 | tf_op jit(solution)/shard_map/ppermute | solution.py:343
  11.5 7.2 %collective-permute-start = (bf16[272,128]{1,0:T(8,128)(2,1)}, bf16[272,128]{1,0:T(8,128)(2,1)S(1)}, u32[]{:S(2)}, u32[]{:S(2)}) collective-permute-start(bf16[272,128]{1,0:T(8,128)(2,1)} %pack.1.own_ref), channel_id=1, source_target_pairs={{0,28},{1,25},{2,30},{3,27},{4,24},{5,29},{6,26},{7,31},{8,20},{9,... | collective-permute-start | bytes 208904 | tf_op jit(solution)/shard_map/ppermute | solution.py:343
  11.5 2.2 %copy-start = (bf16[1,2,1024,1024]{3,2,1,0:T(8,128)(2,1)S(1)}, bf16[1,2,1024,1024]{3,2,1,0:T(8,128)(2,1)}, u32[]{:S(2)}) copy-start(bf16[1,2,1024,1024]{3,2,1,0:T(8,128)(2,1)} %param.8) | copy-start | bytes 12582916
  13.7 6.7 %copy-start.1 = (bf16[272,128]{1,0:T(8,128)(2,1)S(1)}, bf16[272,128]{1,0:T(8,128)(2,1)}, u32[]{:S(2)}) copy-start(bf16[272,128]{1,0:T(8,128)(2,1)} %pack.1.own_ref) | copy-start | bytes 208900
  13.7 6.7 %copy-start.2 = (bf16[1,2,32,1024]{3,2,1,0:T(8,128)(2,1)S(1)}, bf16[1,2,32,1024]{3,2,1,0:T(8,128)(2,1)}, u32[]{:S(2)}) copy-start(bf16[1,2,32,1024]{3,2,1,0:T(8,128)(2,1)} %param.7) | copy-start | bytes 393220
  13.7 6.7 %copy-start.3 = (s32[32,24]{0,1:T(8,128)S(1)}, s32[32,24]{0,1:T(8,128)}, u32[]{:S(2)}) copy-start(s32[32,24]{0,1:T(8,128)} %param.13) | copy-start | bytes 9220
  18.7 1.6 %collective-permute-start.4 = (bf16[1088,128]{1,0:T(8,128)(2,1)S(1)}, bf16[1088,128]{1,0:T(8,128)(2,1)S(1)}, u32[]{:S(2)}, u32[]{:S(2)}) collective-permute-start(bf16[1088,128]{1,0:T(8,128)(2,1)S(1)} %pad_maximum_fusion.direct_ref), channel_id=1, source_target_pairs={{0,1},{1,0},{2,3},{3,2},{4,5},{5,4},{6,7},{7,6},{8,9},{9,8},{10,11... | collective-permute-start | bytes 835592 | tf_op jit(solution)/shard_map/ppermute | solution.py:356

commit v4 on v3

--- a/solution.py
+++ b/solution.py
@@ -13,9 +13,10 @@
 PAD_ROWS = 64
 EXTRA_ROWS = 16
 CODE_BASE = 256
-QUARTER_TURN = 0.6366197723675814
-SIN_TERMS = (1.5707963219600276, -0.6459634781534198, 0.079680222858126, -0.004602163104811149)
-COS_TERMS = (0.9999999723759501, -1.2336970108360321, 0.25359860771245774, -0.020408255467132635)
+HALF_TURN = 0.3183098861837907
+SIN_TERMS = (3.141592640130706, -5.167710083507879, 2.550077523214355, -0.598291285618806, 0.07765766030210168)
+COS_TERMS = (0.9999999532476083, -4.9347928306196405, 4.058411352862505, -1.3318765680803568, 0.2196896110969353)
+TOGETHER = (8, 4, 2)
 VMEM_LIMIT = 24 * 1024 * 1024
 SPREAD_LIMIT = 24 * 1024 * 1024
 
@@ -30,17 +31,16 @@
 def sine_and_cosine(turns):
     nearest = jnp.round(turns)
     rest = turns - nearest
-    quadrant = nearest.astype(jnp.int32)
     square = rest * rest
     sine = polynomial(SIN_TERMS, square) * rest
     cosine = polynomial(COS_TERMS, square)
-    odd = (quadrant & 1) != 0
-    return (
-        jnp.where(odd, cosine, sine),
-        jnp.where(odd, sine, cosine),
-        (quadrant & 2) != 0,
-        ((quadrant + 1) & 2) != 0,
-    )
+    return sine, cosine, (nearest.astype(jnp.int32) & 1) != 0
+
+
+def parity(number):
+    number = number ^ (number >> 4)
+    number = number ^ (number >> 2)
+    return (number ^ (number >> 1)) & 1
 
 
 def pack(env_ref, bottom_ref, out_ref, wide):
@@ -73,7 +73,7 @@
 
 def propagate(
     track_smem, wavenumber_smem, loss_smem, tracks_ref, starter_ref, prop, own_ref, direct_ref, passed_ref,
-    grid_ref, sin_table, cos_table,
+    grid_ref, sin_table, cos_table, bottom_rows,
     field_a, field_b, sin_a, cos_a, sin_b, cos_b, powers,
 ):
     pieces, double_depth, _ = prop.shape
@@ -85,15 +85,13 @@
     columns_here = cell_rows // pieces
     rounds = direct_ref.shape[0] // block_rows
     stride = pieces + 1
-    per_turn = wavenumber_smem[0] * jnp.float32(QUARTER_TURN)
+    per_turn = wavenumber_smem[0] * jnp.float32(HALF_TURN)
     decay = jnp.exp(jnp.full((pieces, LANES), -loss_smem[0], jnp.float32))
     me = lax.axis_index("bearing")
     core = lax.axis_index("freq") % 2
-    owners = 2 * rounds
 
     def place_of(turn, unit):
-        offset = owners - 1 - 2 * turn - unit
-        return jnp.where(offset == 0, owners, me ^ offset)
+        return me ^ (2 * turn + (parity(turn) ^ 1 ^ unit))
 
     depth_index = lax.broadcasted_iota(jnp.int32, (pieces, LANES), 0) * LANES + lax.broadcasted_iota(
         jnp.int32, (pieces, LANES), 1
@@ -104,24 +102,33 @@
         base = place * cell_rows
         codes = ref[pl.ds(start + cell_rows, EXTRA_ROWS), :].astype(jnp.float32)
         bottoms = codes[0:1] * jnp.float32(CODE_BASE) + codes[1:2]
-        bottoms = jnp.broadcast_to(bottoms, (pieces, LANES))
+        own_lane = lax.broadcasted_iota(jnp.int32, (columns_here, LANES), 0) == lax.broadcasted_iota(
+            jnp.int32, (columns_here, LANES), 1
+        )
+        bottoms = jnp.sum(jnp.where(own_lane, bottoms, jnp.float32(0)), axis=1, keepdims=True)
+        bottom_rows[...] = jnp.broadcast_to(bottoms, (columns_here, LANES))
         for pair in range(columns_here // 2):
             both = ref[pl.ds(pl.multiple_of(start + pair * 2 * pieces, 2 * pieces), 2 * pieces), :]
             both = both.astype(jnp.float32) * per_turn
             for column in (2 * pair, 2 * pair + 1):
                 inner = (column - 2 * pair) * pieces
-                sine, cosine, sine_minus, cosine_minus = sine_and_cosine(both[inner : inner + pieces])
-                bottom = jnp.broadcast_to(bottoms[:, column : column + 1], (pieces, LANES))
+                sine, cosine, minus = sine_and_cosine(both[inner : inner + pieces])
+                bottom = bottom_rows[column : column + 1, :]
                 damping = jnp.where(depth_index >= bottom, decay, jnp.float32(1.0))
                 rows = pl.ds(pl.multiple_of(base + column * pieces, pieces), pieces)
-                sin_table[rows, :] = sine * jnp.where(sine_minus, -damping, damping)
-                cos_table[rows, :] = cosine * jnp.where(cosine_minus, -damping, damping)
-
-    tabulate(own_ref, me, 0)
+                damping = jnp.where(minus, -damping, damping)
+                sin_table[rows, :] = sine * damping
+                cos_table[rows, :] = cosine * damping
+
     for index, ref in enumerate((direct_ref, passed_ref)):
 
         def one(turn, carry, ref=ref, index=index):
-            tabulate(ref, place_of(turn, core ^ index), turn * block_rows)
+            place = place_of(turn, core ^ index)
+
+            @pl.when(place != me)
+            def _():
+                tabulate(ref, place, turn * block_rows)
+
             return carry
 
         lax.fori_loop(0, rounds, one, 0)
@@ -180,13 +187,12 @@
                 for tile in early:
                     multiply(field, half, tile)
 
-        def advance(step, field, following, sin_ref, cos_ref, next_sin, next_cos):
+        def advance(step, field, following, sin_ref, cos_ref, next_sin, next_cos, last=False):
             work = [[] for _ in range(slots_of_step + 1)]
             share = -(-bearings // slots_of_step)
-            coming = jnp.minimum(step + 1, steps - 1)
-            for slot in range(slots_of_step):
+            for slot in range(0 if last else slots_of_step):
                 which = range(slot * share, min(bearings, (slot + 1) * share))
-                work[slot].append(functools.partial(prepare, coming, next_sin, next_cos, which))
+                work[slot].append(functools.partial(prepare, step + 1, next_sin, next_cos, which))
             moved = {}
             folded = {}
 
@@ -225,7 +231,8 @@
             for source, order in ((field, late), (following, early)):
                 for half in range(halves):
                     for tile in order:
-                        multiply(source, half, tile)
+                        if source is field or not last:
+                            multiply(source, half, tile)
                         for item in work[slot]:
                             item()
                         slot += 1
@@ -235,18 +242,21 @@
             powers[rows, :] = folded[pieces, 0]
 
         begin(field_a)
+        tabulate(own_ref, me, 0)
         prepare(0, sin_a, cos_a, range(bearings))
 
-        together = 4 if steps % 4 == 0 else 2
-
-        def some_steps(index, carry):
+        together = next(number for number in TOGETHER if steps % number == 0)
+
+        def some_steps(index, carry, last=False):
             for step in range(0, together, 2):
                 advance(index * together + step, field_a, field_b, sin_a, cos_a, sin_b, cos_b)
-                advance(index * together + step + 1, field_b, field_a, sin_b, cos_b, sin_a, cos_a)
+                ends = last and step + 2 == together
+                advance(index * together + step + 1, field_b, field_a, sin_b, cos_b, sin_a, cos_a, ends)
             return carry
 
-        lax.fori_loop(0, steps // together, some_steps, 0)
-        for accumulator in accumulators:
+        lax.fori_loop(0, steps // together - 1, some_steps, 0)
+        some_steps(steps // together - 1, 0, True)
+        for accumulator in spare:
             pltpu.matmul_pop(accumulator)
 
     pl.run_scoped(
@@ -331,7 +341,7 @@
         name="pack",
     )(env_speed, bottom.reshape(1, -1))
 
-    turns = [(offset, offset - 1) for offset in range(owners - 1, 0, -2)]
+    turns = [(2 * turn + 1 - parity(turn), 2 * turn + parity(turn)) for turn in range(owners // 2)]
     received = []
     for turn in turns:
         pairs = [
@@ -362,8 +372,9 @@
         in_specs=[smem] * 3 + [vmem] * 6,
         out_specs=vmem,
         scratch_shapes=[
-            pltpu.VMEM(((owners + 1) * columns_here * pieces, LANES), jnp.float32),
-            pltpu.VMEM(((owners + 1) * columns_here * pieces, LANES), jnp.float32),
+            pltpu.VMEM((owners * columns_here * pieces, LANES), jnp.float32),
+            pltpu.VMEM((owners * columns_here * pieces, LANES), jnp.float32),
+            pltpu.VMEM((columns_here, LANES), jnp.float32),
         ]
         + [pltpu.VMEM((2 * bearings_here, 2 * depth_cells), jnp.bfloat16)] * 2
         + [pltpu.VMEM((bearings_here * (pieces + 1), LANES), jnp.float32)] * 4

time: 51.8 us -> 49.4 us (0.954)
  waiting for transfers between devices: 4.08 us -> 1.01 us
  blocking collectives: 10.6 us -> 13.4 us
  Pallas kernels: 23.2 us -> 22 us
  starting transfers between devices: 10 us -> 9.07 us
    ppermute x4, waiting for transfers between devices: 3.83 us -> 0.76 us  [on_device(): received.append(lax.ppermute(own, ('bearing', 'freq'), pairs))]
    all_to_all x1, blocking collectives: 10.6 us -> 13.4 us  [on_device(): lax.all_to_all(grid.reshape(devices, column_total // devices, bands), ('b...]
    pallas_call x1, Pallas kernels: 18.8 us -> 17.7 us  [on_device(): pl.pallas_call(propagate, out_shape=jax.ShapeDtypeStruct((column_total, b...]
    ppermute x4, starting transfers between devices: 9.97 us -> 9 us  [on_device(): received.append(lax.ppermute(own, ('bearing', 'freq'), pairs))]
  transfers between devices with their start and end apart: 5 -> 5, of which waited for: 3 -> 2; matrix products, arithmetic and copies ran while one was open for 0% -> 0% of each run, Pallas kernels for 2% -> 2%
where the time goes in v4:
time: 49.4 us; the launch traced here: 49.1 us
  Pallas kernels  22 us (45%)
  blocking collectives  13.4 us (27%)
  starting transfers between devices  9.07 us (18%)
  local copies, waits for them, and re-layouts  2.19 us (4%)
  between operations  1.37 us (3%)
  waiting for transfers between devices  1.01 us (2%)
    pallas_call x1, Pallas kernels, on_device(): pl.pallas_call(propagate, out_shape=jax.ShapeDtypeStruct((column_total, b...  17.7 us
    all_to_all x1, blocking collectives, on_device(): lax.all_to_all(grid.reshape(devices, column_total // devices, bands), ('b...  13.4 us
    ppermute x4, starting transfers between devices, on_device(): received.append(lax.ppermute(own, ('bearing', 'freq'), pairs))  9 us
    unnamed x8, local copies, waits for them, and re-layouts  2.19 us
    pallas_call x1, Pallas kernels, on_device(): pl.pallas_call(functools.partial(finish, scale), out_shape=jax.ShapeDtype...  1.67 us
    pallas_call x1, Pallas kernels, on_device(): pl.pallas_call(pack, out_shape=jax.ShapeDtypeStruct((columns_here * piece...  1.5 us
    pallas_call x1, Pallas kernels, on_device(): pl.pallas_call(spread, out_shape=jax.ShapeDtypeStruct((pieces, 2 * depth_...  1.17 us
  transfers between devices with their start and end apart: 5, of which 2 were waited for; matrix products, arithmetic and copies ran while one was open for 0% of the time, Pallas kernels for 2%

profile of v4, /device:TPU:0, one launch (start us, length us, event | category | flops | bytes accessed | tf_op | source)
XLA Modules:
  0.0 49.1 jit_solution(7829022658003154231)
XLA Ops:
  0.0 1.5 %pack.1.own_ref = bf16[272,128]{1,0:T(8,128)(2,1)} custom-call(bf16[32,1024]{1,0:T(8,128)(2,1)} %env_ref.1, s32[1,32]{1,0:T(1,128)} %bitcast.10), custom_call_target="tpu_custom_call" | custom-call | tf_op jit(solution)/shard_map/pack/pallas_call | solution.py:335
  1.5 6.0 %collective-permute-start.3 = (bf16[272,128]{1,0:T(8,128)(2,1)}, bf16[272,128]{1,0:T(8,128)(2,1)S(1)}, u32[]{:S(2)}, u32[]{:S(2)}) collective-permute-start(bf16[272,128]{1,0:T(8,128)(2,1)} %pack.1.own_ref), channel_id=1, source_target_pairs={{0,28},{1,25},{2,30},{3,27},{4,24},{5,29},{6,26},{7,31},{8,20},{9,... | collective-permute-start | bytes 208904 | tf_op jit(solution)/shard_map/ppermute | solution.py:353
  7.5 0.0 collective-permute-start.2
  7.5 0.8 %collective-permute-start.1 = (bf16[272,128]{1,0:T(8,128)(2,1)}, bf16[272,128]{1,0:T(8,128)(2,1)S(1)}, u32[]{:S(2)}, u32[]{:S(2)}) collective-permute-start(bf16[272,128]{1,0:T(8,128)(2,1)} %pack.1.own_ref), channel_id=1, source_target_pairs={{0,8},{1,13},{2,10},{3,15},{4,12},{5,9},{6,14},{7,11},{8,0},{9,5},... | collective-permute-start | bytes 208904 | tf_op jit(solution)/shard_map/ppermute | solution.py:353
  8.3 2.2 %collective-permute-start = (bf16[272,128]{1,0:T(8,128)(2,1)}, bf16[272,128]{1,0:T(8,128)(2,1)S(1)}, u32[]{:S(2)}, u32[]{:S(2)}) collective-permute-start(bf16[272,128]{1,0:T(8,128)(2,1)} %pack.1.own_ref), channel_id=1, source_target_pairs={{0,4},{2,6},{4,0},{6,2},{8,12},{10,14},{12,8},{14,10},{16,20},{18,... | collective-permute-start | bytes 208904 | tf_op jit(solution)/shard_map/ppermute | solution.py:353
  10.5 0.0 copy-start
  10.5 2.2 %copy-done = bf16[1,2,1024,1024]{3,2,1,0:T(8,128)(2,1)S(1)} copy-done((bf16[1,2,1024,1024]{3,2,1,0:T(8,128)(2,1)S(1)}, bf16[1,2,1024,1024]{3,2,1,0:T(8,128)(2,1)}, u32[]{:S(2)}) %copy-start) | copy-done | bytes 4194328
  12.7 0.0 copy-start.1
  12.7 0.0 copy-start.2
  12.7 0.0 copy-start.3
  12.7 1.2 %spread.1.prop = bf16[8,2048,128]{2,1,0:T(8,128)(2,1)S(1)} custom-call(bf16[2048,1024]{1,0:T(8,128)(2,1)S(1)} %bitcast.5), custom_call_target="tpu_custom_call" | custom-call | bytes 8388608 | tf_op jit(solution)/shard_map/spread/pallas_call | solution.py:354
  13.9 0.0 collective-permute-done.3
  13.9 0.0 collective-permute-done.2
  13.9 0.0 collective-permute-done.1
  13.9 0.7 %collective-permute-done = bf16[272,128]{1,0:T(8,128)(2,1)S(1)} collective-permute-done((bf16[272,128]{1,0:T(8,128)(2,1)}, bf16[272,128]{1,0:T(8,128)(2,1)S(1)}, u32[]{:S(2)}, u32[]{:S(2)}) %collective-permute-start) | collective-permute-done | bytes 69664 | tf_op jit(solution)/shard_map/ppermute | solution.py:353
  14.7 0.1 collective-permute-start.4
  16.1 0.3 collective-permute-done.4.passed_ref
  16.3 0.0 copy-done.1
  16.3 0.0 copy-done.2
  16.3 0.0 copy-done.3
  16.3 17.7 %propagate.1 = f32[256,128]{1,0:T(8,128)S(1)} custom-call(s32[24,32]{1,0:T(8,128)S(1)} %bitcast.8, f32[1]{0:T(128)S(6)} %copy.8.wavenumber_smem, f32[1]{0:T(128)S(6)} %copy.9.loss_smem, s32[24,32]{1,0:T(8,128)S(1)} %bitcast.9, bf16[64,1024]{1,0:T(8,128)(2,1)S(1)} %bitcast.7, bf16[8,2048,128]{2,1,0:T(8,128)(2,1)S(1)} %spread.1.prop, ...), custom_call_target="tpu_custom_call" | custom-call | tf_op jit(solution)/shard_map/propagate/pallas_call | solution.py:369
  34.0 13.4 %all_to_all.5.parts_ref = f32[32,8,128]{2,1,0:T(8,128)} all-to-all(f32[32,8,128]{2,1,0:T(8,128)S(1)} %bitcast.6), channel_id=1, replica_groups=mesh['bearing'=8,'freq'=4] {'bearing','freq'}, dimensions={0} | all-to-all | bytes 262144 | tf_op jit(solution)/shard_map/all_to_all | solution.py:388
  47.4 1.7 %finish.1 = f32[8,128]{1,0:T(8,128)} custom-call(f32[32,8,128]{2,1,0:T(8,128)} %all_to_all.5.parts_ref), custom_call_target="tpu_custom_call" | custom-call | tf_op jit(solution)/shard_map/finish/pallas_call | solution.py:392
  (1 shorter events, 0.0 us)
Async XLA Ops:
  1.5 12.4 %collective-permute-start.3 = (bf16[272,128]{1,0:T(8,128)(2,1)}, bf16[272,128]{1,0:T(8,128)(2,1)S(1)}, u32[]{:S(2)}, u32[]{:S(2)}) collective-permute-start(bf16[272,128]{1,0:T(8,128)(2,1)} %pack.1.own_ref), channel_id=1, source_target_pairs={{0,28},{1,25},{2,30},{3,27},{4,24},{5,29},{6,26},{7,31},{8,20},{9,... | collective-permute-start | bytes 208904 | tf_op jit(solution)/shard_map/ppermute | solution.py:353
  7.5 6.4 %collective-permute-start.2 = (bf16[272,128]{1,0:T(8,128)(2,1)}, bf16[272,128]{1,0:T(8,128)(2,1)S(1)}, u32[]{:S(2)}, u32[]{:S(2)}) collective-permute-start(bf16[272,128]{1,0:T(8,128)(2,1)} %pack.1.own_ref), channel_id=1, source_target_pairs={{0,16},{1,21},{2,18},{3,23},{4,20},{5,17},{6,22},{7,19},{8,24},{9,... | collective-permute-start | bytes 208904 | tf_op jit(solution)/shard_map/ppermute | solution.py:353
  7.5 6.4 %collective-permute-start.1 = (bf16[272,128]{1,0:T(8,128)(2,1)}, bf16[272,128]{1,0:T(8,128)(2,1)S(1)}, u32[]{:S(2)}, u32[]{:S(2)}) collective-permute-start(bf16[272,128]{1,0:T(8,128)(2,1)} %pack.1.own_ref), channel_id=1, source_target_pairs={{0,8},{1,13},{2,10},{3,15},{4,12},{5,9},{6,14},{7,11},{8,0},{9,5},... | collective-permute-start | bytes 208904 | tf_op jit(solution)/shard_map/ppermute | solution.py:353
  8.3 6.4 %collective-permute-start = (bf16[272,128]{1,0:T(8,128)(2,1)}, bf16[272,128]{1,0:T(8,128)(2,1)S(1)}, u32[]{:S(2)}, u32[]{:S(2)}) collective-permute-start(bf16[272,128]{1,0:T(8,128)(2,1)} %pack.1.own_ref), channel_id=1, source_target_pairs={{0,4},{2,6},{4,0},{6,2},{8,12},{10,14},{12,8},{14,10},{16,20},{18,... | collective-permute-start | bytes 208904 | tf_op jit(solution)/shard_map/ppermute | solution.py:353
  10.5 2.2 %copy-start = (bf16[1,2,1024,1024]{3,2,1,0:T(8,128)(2,1)S(1)}, bf16[1,2,1024,1024]{3,2,1,0:T(8,128)(2,1)}, u32[]{:S(2)}) copy-start(bf16[1,2,1024,1024]{3,2,1,0:T(8,128)(2,1)} %param.8) | copy-start | bytes 12582916
  12.7 3.6 %copy-start.1 = (bf16[272,128]{1,0:T(8,128)(2,1)S(1)}, bf16[272,128]{1,0:T(8,128)(2,1)}, u32[]{:S(2)}) copy-start(bf16[272,128]{1,0:T(8,128)(2,1)} %pack.1.own_ref) | copy-start | bytes 208900
  12.7 3.6 %copy-start.2 = (bf16[1,2,32,1024]{3,2,1,0:T(8,128)(2,1)S(1)}, bf16[1,2,32,1024]{3,2,1,0:T(8,128)(2,1)}, u32[]{:S(2)}) copy-start(bf16[1,2,32,1024]{3,2,1,0:T(8,128)(2,1)} %param.7) | copy-start | bytes 393220
  12.7 3.6 %copy-start.3 = (s32[32,24]{0,1:T(8,128)S(1)}, s32[32,24]{0,1:T(8,128)}, u32[]{:S(2)}) copy-start(s32[32,24]{0,1:T(8,128)} %param.13) | copy-start | bytes 9220
  14.7 1.6 %collective-permute-start.4 = (bf16[1088,128]{1,0:T(8,128)(2,1)S(1)}, bf16[1088,128]{1,0:T(8,128)(2,1)S(1)}, u32[]{:S(2)}, u32[]{:S(2)}) collective-permute-start(bf16[1088,128]{1,0:T(8,128)(2,1)S(1)} %pad_maximum_fusion.direct_ref), channel_id=1, source_target_pairs={{0,1},{1,0},{2,3},{3,2},{4,5},{5,4},{6,7},{7,6},{8,9},{9,8},{10,11... | collective-permute-start | bytes 835592 | tf_op jit(solution)/shard_map/ppermute | solution.py:366

commit v5 on v4

--- a/solution.py
+++ b/solution.py
@@ -72,6 +72,7 @@
 
 
 def propagate(
+    turns,
     track_smem, wavenumber_smem, loss_smem, tracks_ref, starter_ref, prop, own_ref, direct_ref, passed_ref,
     grid_ref, sin_table, cos_table, bottom_rows,
     field_a, field_b, sin_a, cos_a, sin_b, cos_b, powers,
@@ -91,7 +92,10 @@
     core = lax.axis_index("freq") % 2
 
     def place_of(turn, unit):
-        return me ^ (2 * turn + (parity(turn) ^ 1 ^ unit))
+        offset = jnp.int32(0)
+        for index, pair in enumerate(turns):
+            offset = jnp.where(turn == index, jnp.where(unit == 0, pair[0], pair[1]), offset)
+        return me ^ offset
 
     depth_index = lax.broadcasted_iota(jnp.int32, (pieces, LANES), 0) * LANES + lax.broadcasted_iota(
         jnp.int32, (pieces, LANES), 1
@@ -341,7 +345,10 @@
         name="pack",
     )(env_speed, bottom.reshape(1, -1))
 
-    turns = [(2 * turn + 1 - parity(turn), 2 * turn + parity(turn)) for turn in range(owners // 2)]
+    odd = [offset for offset in range(owners) if parity(offset)]
+    even = [offset for offset in range(owners) if not parity(offset)]
+    odd[-2:] = odd[:-3:-1]
+    turns = list(zip(odd, even))
     received = []
     for turn in turns:
         pairs = [
@@ -367,7 +374,7 @@
 
     tracks = track_column.T
     grid = pl.pallas_call(
-        propagate,
+        functools.partial(propagate, turns),
         out_shape=jax.ShapeDtypeStruct((column_total, bands), jnp.float32),
         in_specs=[smem] * 3 + [vmem] * 6,
         out_specs=vmem,

time: 49.4 us -> 48.5 us (0.982)
  no operation moved by 1% of the time
where the time goes in v5:
time: 48.5 us; the launch traced here: 48.2 us
  Pallas kernels  22 us (45%)
  blocking collectives  13 us (27%)
  starting transfers between devices  9.07 us (19%)
  local copies, waits for them, and re-layouts  2.19 us (5%)
  between operations  1.37 us (3%)
  waiting for transfers between devices  0.56 us (1%)
    pallas_call x1, Pallas kernels, on_device(): pl.pallas_call(functools.partial(propagate, turns), out_shape=jax.ShapeDt...  17.6 us
    all_to_all x1, blocking collectives, on_device(): lax.all_to_all(grid.reshape(devices, column_total // devices, bands), ('b...  13 us
    ppermute x4, starting transfers between devices, on_device(): received.append(lax.ppermute(own, ('bearing', 'freq'), pairs))  9 us
    unnamed x8, local copies, waits for them, and re-layouts  2.19 us
    pallas_call x1, Pallas kernels, on_device(): pl.pallas_call(functools.partial(finish, scale), out_shape=jax.ShapeDtype...  1.67 us
    pallas_call x1, Pallas kernels, on_device(): pl.pallas_call(pack, out_shape=jax.ShapeDtypeStruct((columns_here * piece...  1.5 us
    pallas_call x1, Pallas kernels, on_device(): pl.pallas_call(spread, out_shape=jax.ShapeDtypeStruct((pieces, 2 * depth_...  1.17 us
  transfers between devices with their start and end apart: 5, of which 2 were waited for; matrix products, arithmetic and copies ran while one was open for 0% of the time, Pallas kernels for 2%

profile of v5, /device:TPU:0, one launch (start us, length us, event | category | flops | bytes accessed | tf_op | source)
XLA Modules:
  0.0 48.2 jit_solution(5961932573503816871)
XLA Ops:
  0.0 1.5 %pack.1.own_ref = bf16[272,128]{1,0:T(8,128)(2,1)} custom-call(bf16[32,1024]{1,0:T(8,128)(2,1)} %env_ref.1, s32[1,32]{1,0:T(1,128)} %bitcast.10), custom_call_target="tpu_custom_call" | custom-call | tf_op jit(solution)/shard_map/pack/pallas_call | solution.py:339
  1.5 4.0 %collective-permute-start.3 = (bf16[272,128]{1,0:T(8,128)(2,1)}, bf16[272,128]{1,0:T(8,128)(2,1)S(1)}, u32[]{:S(2)}, u32[]{:S(2)}) collective-permute-start(bf16[272,128]{1,0:T(8,128)(2,1)} %pack.1.own_ref), channel_id=1, source_target_pairs={{0,16},{1,25},{2,18},{3,27},{4,20},{5,29},{6,22},{7,31},{8,24},{9,... | collective-permute-start | bytes 208904 | tf_op jit(solution)/shard_map/ppermute | solution.py:360
  5.5 2.3 %collective-permute-start.2 = (bf16[272,128]{1,0:T(8,128)(2,1)}, bf16[272,128]{1,0:T(8,128)(2,1)S(1)}, u32[]{:S(2)}, u32[]{:S(2)}) collective-permute-start(bf16[272,128]{1,0:T(8,128)(2,1)} %pack.1.own_ref), channel_id=1, source_target_pairs={{0,28},{1,21},{2,30},{3,23},{4,24},{5,17},{6,26},{7,19},{8,20},{9,... | collective-permute-start | bytes 208904 | tf_op jit(solution)/shard_map/ppermute | solution.py:360
  7.8 0.0 collective-permute-start.1
  7.8 2.7 %collective-permute-start = (bf16[272,128]{1,0:T(8,128)(2,1)}, bf16[272,128]{1,0:T(8,128)(2,1)S(1)}, u32[]{:S(2)}, u32[]{:S(2)}) collective-permute-start(bf16[272,128]{1,0:T(8,128)(2,1)} %pack.1.own_ref), channel_id=1, source_target_pairs={{0,4},{2,6},{4,0},{6,2},{8,12},{10,14},{12,8},{14,10},{16,20},{18,... | collective-permute-start | bytes 208904 | tf_op jit(solution)/shard_map/ppermute | solution.py:360
  10.5 0.0 copy-start
  10.5 2.2 %copy-done = bf16[1,2,1024,1024]{3,2,1,0:T(8,128)(2,1)S(1)} copy-done((bf16[1,2,1024,1024]{3,2,1,0:T(8,128)(2,1)S(1)}, bf16[1,2,1024,1024]{3,2,1,0:T(8,128)(2,1)}, u32[]{:S(2)}) %copy-start) | copy-done | bytes 4194328
  12.7 0.0 copy-start.1
  12.7 0.0 copy-start.2
  12.7 0.0 copy-start.3
  12.7 1.2 %spread.1.prop = bf16[8,2048,128]{2,1,0:T(8,128)(2,1)S(1)} custom-call(bf16[2048,1024]{1,0:T(8,128)(2,1)S(1)} %bitcast.5), custom_call_target="tpu_custom_call" | custom-call | bytes 8388608 | tf_op jit(solution)/shard_map/spread/pallas_call | solution.py:361
  13.9 0.0 collective-permute-done.3
  13.9 0.0 collective-permute-done.2
  13.9 0.0 collective-permute-done.1
  13.9 0.3 collective-permute-done
  14.2 0.1 collective-permute-start.4
  15.6 0.3 collective-permute-done.4.passed_ref
  15.9 0.0 copy-done.1
  15.9 0.0 copy-done.2
  15.9 0.0 copy-done.3
  15.9 17.6 %propagate.1 = f32[256,128]{1,0:T(8,128)S(1)} custom-call(s32[24,32]{1,0:T(8,128)S(1)} %bitcast.8, f32[1]{0:T(128)S(6)} %copy.8.wavenumber_smem, f32[1]{0:T(128)S(6)} %copy.9.loss_smem, s32[24,32]{1,0:T(8,128)S(1)} %bitcast.9, bf16[64,1024]{1,0:T(8,128)(2,1)S(1)} %bitcast.7, bf16[8,2048,128]{2,1,0:T(8,128)(2,1)S(1)} %spread.1.prop, ...), custom_call_target="tpu_custom_call" | custom-call | tf_op jit(solution)/shard_map/propagate/pallas_call | solution.py:376
  33.5 13.0 %all_to_all.5.parts_ref = f32[32,8,128]{2,1,0:T(8,128)} all-to-all(f32[32,8,128]{2,1,0:T(8,128)S(1)} %bitcast.6), channel_id=1, replica_groups=mesh['bearing'=8,'freq'=4] {'bearing','freq'}, dimensions={0} | all-to-all | bytes 262144 | tf_op jit(solution)/shard_map/all_to_all | solution.py:395
  46.6 1.7 %finish.1 = f32[8,128]{1,0:T(8,128)} custom-call(f32[32,8,128]{2,1,0:T(8,128)} %all_to_all.5.parts_ref), custom_call_target="tpu_custom_call" | custom-call | tf_op jit(solution)/shard_map/finish/pallas_call | solution.py:399
  (1 shorter events, 0.0 us)
Async XLA Ops:
  1.5 12.4 %collective-permute-start.3 = (bf16[272,128]{1,0:T(8,128)(2,1)}, bf16[272,128]{1,0:T(8,128)(2,1)S(1)}, u32[]{:S(2)}, u32[]{:S(2)}) collective-permute-start(bf16[272,128]{1,0:T(8,128)(2,1)} %pack.1.own_ref), channel_id=1, source_target_pairs={{0,16},{1,25},{2,18},{3,27},{4,20},{5,29},{6,22},{7,31},{8,24},{9,... | collective-permute-start | bytes 208904 | tf_op jit(solution)/shard_map/ppermute | solution.py:360
  5.5 8.4 %collective-permute-start.2 = (bf16[272,128]{1,0:T(8,128)(2,1)}, bf16[272,128]{1,0:T(8,128)(2,1)S(1)}, u32[]{:S(2)}, u32[]{:S(2)}) collective-permute-start(bf16[272,128]{1,0:T(8,128)(2,1)} %pack.1.own_ref), channel_id=1, source_target_pairs={{0,28},{1,21},{2,30},{3,23},{4,24},{5,17},{6,26},{7,19},{8,20},{9,... | collective-permute-start | bytes 208904 | tf_op jit(solution)/shard_map/ppermute | solution.py:360
  7.8 6.1 %collective-permute-start.1 = (bf16[272,128]{1,0:T(8,128)(2,1)}, bf16[272,128]{1,0:T(8,128)(2,1)S(1)}, u32[]{:S(2)}, u32[]{:S(2)}) collective-permute-start(bf16[272,128]{1,0:T(8,128)(2,1)} %pack.1.own_ref), channel_id=1, source_target_pairs={{0,8},{1,13},{2,10},{3,15},{4,12},{5,9},{6,14},{7,11},{8,0},{9,5},... | collective-permute-start | bytes 208904 | tf_op jit(solution)/shard_map/ppermute | solution.py:360
  7.8 6.4 %collective-permute-start = (bf16[272,128]{1,0:T(8,128)(2,1)}, bf16[272,128]{1,0:T(8,128)(2,1)S(1)}, u32[]{:S(2)}, u32[]{:S(2)}) collective-permute-start(bf16[272,128]{1,0:T(8,128)(2,1)} %pack.1.own_ref), channel_id=1, source_target_pairs={{0,4},{2,6},{4,0},{6,2},{8,12},{10,14},{12,8},{14,10},{16,20},{18,... | collective-permute-start | bytes 208904 | tf_op jit(solution)/shard_map/ppermute | solution.py:360
  10.5 2.2 %copy-start = (bf16[1,2,1024,1024]{3,2,1,0:T(8,128)(2,1)S(1)}, bf16[1,2,1024,1024]{3,2,1,0:T(8,128)(2,1)}, u32[]{:S(2)}) copy-start(bf16[1,2,1024,1024]{3,2,1,0:T(8,128)(2,1)} %param.8) | copy-start | bytes 12582916
  12.7 3.2 %copy-start.1 = (bf16[272,128]{1,0:T(8,128)(2,1)S(1)}, bf16[272,128]{1,0:T(8,128)(2,1)}, u32[]{:S(2)}) copy-start(bf16[272,128]{1,0:T(8,128)(2,1)} %pack.1.own_ref) | copy-start | bytes 208900
  12.7 3.2 %copy-start.2 = (bf16[1,2,32,1024]{3,2,1,0:T(8,128)(2,1)S(1)}, bf16[1,2,32,1024]{3,2,1,0:T(8,128)(2,1)}, u32[]{:S(2)}) copy-start(bf16[1,2,32,1024]{3,2,1,0:T(8,128)(2,1)} %param.7) | copy-start | bytes 393220
  12.7 3.2 %copy-start.3 = (s32[32,24]{0,1:T(8,128)S(1)}, s32[32,24]{0,1:T(8,128)}, u32[]{:S(2)}) copy-start(s32[32,24]{0,1:T(8,128)} %param.13) | copy-start | bytes 9220
  14.2 1.6 %collective-permute-start.4 = (bf16[1088,128]{1,0:T(8,128)(2,1)S(1)}, bf16[1088,128]{1,0:T(8,128)(2,1)S(1)}, u32[]{:S(2)}, u32[]{:S(2)}) collective-permute-start(bf16[1088,128]{1,0:T(8,128)(2,1)S(1)} %pad_maximum_fusion.direct_ref), channel_id=1, source_target_pairs={{0,1},{1,0},{2,3},{3,2},{4,5},{5,4},{6,7},{7,6},{8,9},{9,8},{10,11... | collective-permute-start | bytes 835592 | tf_op jit(solution)/shard_map/ppermute | solution.py:373

commit v6 on v5

--- a/solution.py
+++ b/solution.py
@@ -35,12 +35,6 @@
     sine = polynomial(SIN_TERMS, square) * rest
     cosine = polynomial(COS_TERMS, square)
     return sine, cosine, (nearest.astype(jnp.int32) & 1) != 0
-
-
-def parity(number):
-    number = number ^ (number >> 4)
-    number = number ^ (number >> 2)
-    return (number ^ (number >> 1)) & 1
 
 
 def pack(env_ref, bottom_ref, out_ref, wide):
@@ -345,10 +339,10 @@
         name="pack",
     )(env_speed, bottom.reshape(1, -1))
 
-    odd = [offset for offset in range(owners) if parity(offset)]
-    even = [offset for offset in range(owners) if not parity(offset)]
-    odd[-2:] = odd[:-3:-1]
-    turns = list(zip(odd, even))
+    middle = owners // 2
+    near = [*range(2, middle), middle, 1]
+    far = [*range(middle + 1, owners), 0]
+    turns = list(zip(near, far))[::-1]
     received = []
     for turn in turns:
         pairs = [

time: 48.5 us -> 47.6 us (0.981)
  blocking collectives: 13 us -> 11.5 us
    all_to_all x1, blocking collectives: 13 us -> 11.5 us  [on_device(): lax.all_to_all(grid.reshape(devices, column_total // devices, bands), ('b...]
where the time goes in v6:
time: 47.6 us; the launch traced here: 47.3 us
  Pallas kernels  22 us (46%)
  blocking collectives  11.5 us (24%)
  starting transfers between devices  9.49 us (20%)
  local copies, waits for them, and re-layouts  2.19 us (5%)
  between operations  1.37 us (3%)
  waiting for transfers between devices  0.82 us (2%)
    pallas_call x1, Pallas kernels, on_device(): pl.pallas_call(functools.partial(propagate, turns), out_shape=jax.ShapeDt...  17.6 us
    all_to_all x1, blocking collectives, on_device(): lax.all_to_all(grid.reshape(devices, column_total // devices, bands), ('b...  11.5 us
    ppermute x4, starting transfers between devices, on_device(): received.append(lax.ppermute(own, ('bearing', 'freq'), pairs))  9.42 us
    unnamed x8, local copies, waits for them, and re-layouts  2.19 us
    pallas_call x1, Pallas kernels, on_device(): pl.pallas_call(functools.partial(finish, scale), out_shape=jax.ShapeDtype...  1.67 us
    pallas_call x1, Pallas kernels, on_device(): pl.pallas_call(pack, out_shape=jax.ShapeDtypeStruct((columns_here * piece...  1.5 us
    pallas_call x1, Pallas kernels, on_device(): pl.pallas_call(spread, out_shape=jax.ShapeDtypeStruct((pieces, 2 * depth_...  1.17 us
  transfers between devices with their start and end apart: 5, of which 2 were waited for; matrix products, arithmetic and copies ran while one was open for 0% of the time, Pallas kernels for 2%

profile of v6, /device:TPU:0, one launch (start us, length us, event | category | flops | bytes accessed | tf_op | source)
XLA Modules:
  0.0 47.3 jit_solution(16825317751197183200)
XLA Ops:
  0.0 1.5 %pack.1.own_ref = bf16[272,128]{1,0:T(8,128)(2,1)} custom-call(bf16[32,1024]{1,0:T(8,128)(2,1)} %env_ref.1, s32[1,32]{1,0:T(1,128)} %bitcast.10), custom_call_target="tpu_custom_call" | custom-call | tf_op jit(solution)/shard_map/pack/pallas_call | solution.py:333
  1.5 3.0 %collective-permute-start.3 = (bf16[272,128]{1,0:T(8,128)(2,1)}, bf16[272,128]{1,0:T(8,128)(2,1)S(1)}, u32[]{:S(2)}, u32[]{:S(2)}) collective-permute-start(bf16[272,128]{1,0:T(8,128)(2,1)} %pack.1.own_ref), channel_id=1, source_target_pairs={{0,8},{1,21},{2,10},{3,23},{4,12},{5,17},{6,14},{7,19},{8,0},{9,29... | collective-permute-start | bytes 208904 | tf_op jit(solution)/shard_map/ppermute | solution.py:354
  4.5 1.4 %collective-permute-start.2 = (bf16[272,128]{1,0:T(8,128)(2,1)}, bf16[272,128]{1,0:T(8,128)(2,1)S(1)}, u32[]{:S(2)}, u32[]{:S(2)}) collective-permute-start(bf16[272,128]{1,0:T(8,128)(2,1)} %pack.1.own_ref), channel_id=1, source_target_pairs={{0,12},{1,25},{2,14},{3,27},{4,8},{5,29},{6,10},{7,31},{8,4},{9,17... | collective-permute-start | bytes 208904 | tf_op jit(solution)/shard_map/ppermute | solution.py:354
  5.9 2.6 %collective-permute-start.1 = (bf16[272,128]{1,0:T(8,128)(2,1)}, bf16[272,128]{1,0:T(8,128)(2,1)S(1)}, u32[]{:S(2)}, u32[]{:S(2)}) collective-permute-start(bf16[272,128]{1,0:T(8,128)(2,1)} %pack.1.own_ref), channel_id=1, source_target_pairs={{0,16},{1,29},{2,18},{3,31},{4,20},{5,25},{6,22},{7,27},{8,24},{9,... | collective-permute-start | bytes 208904 | tf_op jit(solution)/shard_map/ppermute | solution.py:354
  8.5 2.4 %collective-permute-start = (bf16[272,128]{1,0:T(8,128)(2,1)}, bf16[272,128]{1,0:T(8,128)(2,1)S(1)}, u32[]{:S(2)}, u32[]{:S(2)}) collective-permute-start(bf16[272,128]{1,0:T(8,128)(2,1)} %pack.1.own_ref), channel_id=1, source_target_pairs={{0,4},{2,6},{4,0},{6,2},{8,12},{10,14},{12,8},{14,10},{16,20},{18,... | collective-permute-start | bytes 208904 | tf_op jit(solution)/shard_map/ppermute | solution.py:354
  10.9 0.0 copy-start
  10.9 2.2 %copy-done = bf16[1,2,1024,1024]{3,2,1,0:T(8,128)(2,1)S(1)} copy-done((bf16[1,2,1024,1024]{3,2,1,0:T(8,128)(2,1)S(1)}, bf16[1,2,1024,1024]{3,2,1,0:T(8,128)(2,1)}, u32[]{:S(2)}) %copy-start) | copy-done | bytes 4194328
  13.1 0.0 copy-start.1
  13.1 0.0 copy-start.2
  13.1 0.0 copy-start.3
  13.1 1.2 %spread.1.prop = bf16[8,2048,128]{2,1,0:T(8,128)(2,1)S(1)} custom-call(bf16[2048,1024]{1,0:T(8,128)(2,1)S(1)} %bitcast.5), custom_call_target="tpu_custom_call" | custom-call | bytes 8388608 | tf_op jit(solution)/shard_map/spread/pallas_call | solution.py:355
  14.3 0.0 collective-permute-done.3
  14.3 0.0 collective-permute-done.2
  14.3 0.0 collective-permute-done.1
  14.3 0.6 %collective-permute-done = bf16[272,128]{1,0:T(8,128)(2,1)S(1)} collective-permute-done((bf16[272,128]{1,0:T(8,128)(2,1)}, bf16[272,128]{1,0:T(8,128)(2,1)S(1)}, u32[]{:S(2)}, u32[]{:S(2)}) %collective-permute-start) | collective-permute-done | bytes 69664 | tf_op jit(solution)/shard_map/ppermute | solution.py:354
  14.9 0.1 collective-permute-start.4
  16.3 0.3 collective-permute-done.4.passed_ref
  16.5 0.0 copy-done.1
  16.5 0.0 copy-done.2
  16.6 0.0 copy-done.3
  16.6 17.6 %propagate.1 = f32[256,128]{1,0:T(8,128)S(1)} custom-call(s32[24,32]{1,0:T(8,128)S(1)} %bitcast.8, f32[1]{0:T(128)S(6)} %copy.8.wavenumber_smem, f32[1]{0:T(128)S(6)} %copy.9.loss_smem, s32[24,32]{1,0:T(8,128)S(1)} %bitcast.9, bf16[64,1024]{1,0:T(8,128)(2,1)S(1)} %bitcast.7, bf16[8,2048,128]{2,1,0:T(8,128)(2,1)S(1)} %spread.1.prop, ...), custom_call_target="tpu_custom_call" | custom-call | tf_op jit(solution)/shard_map/propagate/pallas_call | solution.py:370
  34.2 11.5 %all_to_all.5.parts_ref = f32[32,8,128]{2,1,0:T(8,128)} all-to-all(f32[32,8,128]{2,1,0:T(8,128)S(1)} %bitcast.6), channel_id=1, replica_groups=mesh['bearing'=8,'freq'=4] {'bearing','freq'}, dimensions={0} | all-to-all | bytes 262144 | tf_op jit(solution)/shard_map/all_to_all | solution.py:389
  45.7 1.7 %finish.1 = f32[8,128]{1,0:T(8,128)} custom-call(f32[32,8,128]{2,1,0:T(8,128)} %all_to_all.5.parts_ref), custom_call_target="tpu_custom_call" | custom-call | tf_op jit(solution)/shard_map/finish/pallas_call | solution.py:393
  (1 shorter events, 0.0 us)
Async XLA Ops:
  1.5 12.8 %collective-permute-start.3 = (bf16[272,128]{1,0:T(8,128)(2,1)}, bf16[272,128]{1,0:T(8,128)(2,1)S(1)}, u32[]{:S(2)}, u32[]{:S(2)}) collective-permute-start(bf16[272,128]{1,0:T(8,128)(2,1)} %pack.1.own_ref), channel_id=1, source_target_pairs={{0,8},{1,21},{2,10},{3,23},{4,12},{5,17},{6,14},{7,19},{8,0},{9,29... | collective-permute-start | bytes 208904 | tf_op jit(solution)/shard_map/ppermute | solution.py:354
  4.5 9.8 %collective-permute-start.2 = (bf16[272,128]{1,0:T(8,128)(2,1)}, bf16[272,128]{1,0:T(8,128)(2,1)S(1)}, u32[]{:S(2)}, u32[]{:S(2)}) collective-permute-start(bf16[272,128]{1,0:T(8,128)(2,1)} %pack.1.own_ref), channel_id=1, source_target_pairs={{0,12},{1,25},{2,14},{3,27},{4,8},{5,29},{6,10},{7,31},{8,4},{9,17... | collective-permute-start | bytes 208904 | tf_op jit(solution)/shard_map/ppermute | solution.py:354
  5.9 8.4 %collective-permute-start.1 = (bf16[272,128]{1,0:T(8,128)(2,1)}, bf16[272,128]{1,0:T(8,128)(2,1)S(1)}, u32[]{:S(2)}, u32[]{:S(2)}) collective-permute-start(bf16[272,128]{1,0:T(8,128)(2,1)} %pack.1.own_ref), channel_id=1, source_target_pairs={{0,16},{1,29},{2,18},{3,31},{4,20},{5,25},{6,22},{7,27},{8,24},{9,... | collective-permute-start | bytes 208904 | tf_op jit(solution)/shard_map/ppermute | solution.py:354
  8.5 6.4 %collective-permute-start = (bf16[272,128]{1,0:T(8,128)(2,1)}, bf16[272,128]{1,0:T(8,128)(2,1)S(1)}, u32[]{:S(2)}, u32[]{:S(2)}) collective-permute-start(bf16[272,128]{1,0:T(8,128)(2,1)} %pack.1.own_ref), channel_id=1, source_target_pairs={{0,4},{2,6},{4,0},{6,2},{8,12},{10,14},{12,8},{14,10},{16,20},{18,... | collective-permute-start | bytes 208904 | tf_op jit(solution)/shard_map/ppermute | solution.py:354
  10.9 2.2 %copy-start = (bf16[1,2,1024,1024]{3,2,1,0:T(8,128)(2,1)S(1)}, bf16[1,2,1024,1024]{3,2,1,0:T(8,128)(2,1)}, u32[]{:S(2)}) copy-start(bf16[1,2,1024,1024]{3,2,1,0:T(8,128)(2,1)} %param.8) | copy-start | bytes 12582916
  13.1 3.4 %copy-start.1 = (bf16[272,128]{1,0:T(8,128)(2,1)S(1)}, bf16[272,128]{1,0:T(8,128)(2,1)}, u32[]{:S(2)}) copy-start(bf16[272,128]{1,0:T(8,128)(2,1)} %pack.1.own_ref) | copy-start | bytes 208900
  13.1 3.4 %copy-start.2 = (bf16[1,2,32,1024]{3,2,1,0:T(8,128)(2,1)S(1)}, bf16[1,2,32,1024]{3,2,1,0:T(8,128)(2,1)}, u32[]{:S(2)}) copy-start(bf16[1,2,32,1024]{3,2,1,0:T(8,128)(2,1)} %param.7) | copy-start | bytes 393220
  13.1 3.4 %copy-start.3 = (s32[32,24]{0,1:T(8,128)S(1)}, s32[32,24]{0,1:T(8,128)}, u32[]{:S(2)}) copy-start(s32[32,24]{0,1:T(8,128)} %param.13) | copy-start | bytes 9220
  14.9 1.6 %collective-permute-start.4 = (bf16[1088,128]{1,0:T(8,128)(2,1)S(1)}, bf16[1088,128]{1,0:T(8,128)(2,1)S(1)}, u32[]{:S(2)}, u32[]{:S(2)}) collective-permute-start(bf16[1088,128]{1,0:T(8,128)(2,1)S(1)} %pad_maximum_fusion.direct_ref), channel_id=1, source_target_pairs={{0,1},{1,0},{2,3},{3,2},{4,5},{5,4},{6,7},{7,6},{8,9},{9,8},{10,11... | collective-permute-start | bytes 835592 | tf_op jit(solution)/shard_map/ppermute | solution.py:367

commit v7 on v6

--- a/solution.py
+++ b/solution.py
@@ -69,7 +69,7 @@
     turns,
     track_smem, wavenumber_smem, loss_smem, tracks_ref, starter_ref, prop, own_ref, direct_ref, passed_ref,
     grid_ref, sin_table, cos_table, bottom_rows,
-    field_a, field_b, sin_a, cos_a, sin_b, cos_b, powers,
+    field_a, field_b, sin_a, cos_a, sin_b, cos_b, powers, chosen,
 ):
     pieces, double_depth, _ = prop.shape
     depth_cells = double_depth // 2
@@ -164,6 +164,26 @@
     slots_of_step = halves * (len(early) + len(late))
     nothing = jnp.zeros((PAD_ROWS, TILE), jnp.bfloat16)
 
+    group = TILE // bearings
+    lanes_of_row = lax.broadcasted_iota(jnp.int32, (1, LANES), 1)
+
+    def ids_of(first):
+        parts = []
+        for start in range(first, first + group, LANES // bearings):
+            row = tracks_ref[start : start + 1, :]
+            total = jnp.concatenate([row, jnp.zeros((1, LANES - bearings), jnp.int32)], axis=1)
+            for index in range(1, LANES // bearings):
+                row = tracks_ref[start + index : start + index + 1, :]
+                row = jnp.concatenate([row, jnp.zeros((1, LANES - bearings), jnp.int32)], axis=1)
+                total = total + pltpu.roll(row, index * bearings, 1)
+            parts.append(total)
+        return jnp.concatenate(parts, axis=1)
+
+    def choose():
+        column = lax.broadcasted_iota(jnp.int32, (column_total, TILE), 0)
+        for index, start in enumerate(range(0, steps, group)):
+            chosen[:, index * TILE : (index + 1) * TILE] = (column == ids_of(start)).astype(jnp.bfloat16)
+
     def run(*accumulators):
         sums, spare = accumulators[: 2 * halves], accumulators[2 * halves :]
         count = [0]
@@ -253,6 +273,7 @@
             return carry
 
         lax.fori_loop(0, steps // together - 1, some_steps, 0)
+        choose()
         some_steps(steps // together - 1, 0, True)
         for accumulator in spare:
             pltpu.matmul_pop(accumulator)
@@ -263,26 +284,10 @@
         *[pltpu.ACC(unit)((PAD_ROWS, TILE), jnp.float32) for unit in range(2)],
     )
 
-    group = TILE // bearings
-    lanes_of_row = lax.broadcasted_iota(jnp.int32, (1, LANES), 1)
-
-    def ids_of(first):
-        parts = []
-        for start in range(first, first + group, LANES // bearings):
-            row = tracks_ref[start : start + 1, :]
-            total = jnp.concatenate([row, jnp.zeros((1, LANES - bearings), jnp.int32)], axis=1)
-            for index in range(1, LANES // bearings):
-                row = tracks_ref[start + index : start + index + 1, :]
-                row = jnp.concatenate([row, jnp.zeros((1, LANES - bearings), jnp.int32)], axis=1)
-                total = total + pltpu.roll(row, index * bearings, 1)
-            parts.append(total)
-        return jnp.concatenate(parts, axis=1)
-
     half_columns = column_total // 2
 
     def scatter(*sums):
         for index, start in enumerate(range(0, steps, group)):
-            ids = ids_of(start)
             value = powers[start * bearings : (start + group) * bearings, :]
             high = value.astype(jnp.bfloat16)
             low = (value - high.astype(jnp.float32)).astype(jnp.bfloat16)
@@ -290,9 +295,9 @@
             for unit in range(2):
                 pltpu.matmul_push_rhs(both, index % 2, unit)
             for unit in range(2):
-                column = lax.broadcasted_iota(jnp.int32, (half_columns, TILE), 0) + unit * half_columns
-                chosen = (column == ids).astype(jnp.bfloat16)
-                pltpu.matmul_acc_lhs(sums[unit], chosen, load_staged_rhs=index % 2)
+                rows = slice(unit * half_columns, (unit + 1) * half_columns)
+                cells = slice(index * TILE, (index + 1) * TILE)
+                pltpu.matmul_acc_lhs(sums[unit], chosen[rows, cells], load_staged_rhs=index % 2)
         for unit in range(2):
             total = pltpu.matmul_pop(sums[unit])
             grid_ref[unit * half_columns : (unit + 1) * half_columns, :] = total[:, :LANES] + total[:, LANES:]
@@ -379,7 +384,8 @@
         ]
         + [pltpu.VMEM((2 * bearings_here, 2 * depth_cells), jnp.bfloat16)] * 2
         + [pltpu.VMEM((bearings_here * (pieces + 1), LANES), jnp.float32)] * 4
-        + [pltpu.VMEM((steps * bearings_here, bands), jnp.float32)],
+        + [pltpu.VMEM((steps * bearings_here, bands), jnp.float32)]
+        + [pltpu.VMEM((column_total, steps * bearings_here), jnp.bfloat16)],
         compiler_params=pltpu.CompilerParams(vmem_limit_bytes=VMEM_LIMIT),
         name="propagate",
     )(

time: 47.6 us -> 47.6 us (level)
  no operation moved by 1% of the time
where the time goes in v7:
time: 47.6 us; the launch traced here: 47.3 us
  Pallas kernels  22 us (46%)
  blocking collectives  11.4 us (24%)
  starting transfers between devices  9.49 us (20%)
  local copies, waits for them, and re-layouts  2.19 us (5%)
  between operations  1.37 us (3%)
  waiting for transfers between devices  0.82 us (2%)
    pallas_call x1, Pallas kernels, on_device(): pl.pallas_call(functools.partial(propagate, turns), out_shape=jax.ShapeDt...  17.7 us
    all_to_all x1, blocking collectives, on_device(): lax.all_to_all(grid.reshape(devices, column_total // devices, bands), ('b...  11.4 us
    ppermute x4, starting transfers between devices, on_device(): received.append(lax.ppermute(own, ('bearing', 'freq'), pairs))  9.42 us
    unnamed x8, local copies, waits for them, and re-layouts  2.19 us
    pallas_call x1, Pallas kernels, on_device(): pl.pallas_call(functools.partial(finish, scale), out_shape=jax.ShapeDtype...  1.67 us
    pallas_call x1, Pallas kernels, on_device(): pl.pallas_call(pack, out_shape=jax.ShapeDtypeStruct((columns_here * piece...  1.5 us
    pallas_call x1, Pallas kernels, on_device(): pl.pallas_call(spread, out_shape=jax.ShapeDtypeStruct((pieces, 2 * depth_...  1.17 us
  transfers between devices with their start and end apart: 5, of which 2 were waited for; matrix products, arithmetic and copies ran while one was open for 0% of the time, Pallas kernels for 2%

profile of v7, /device:TPU:0, one launch (start us, length us, event | category | flops | bytes accessed | tf_op | source)
XLA Modules:
  0.0 47.3 jit_solution(11782822560223980381)
XLA Ops:
  0.0 1.5 %pack.1.own_ref = bf16[272,128]{1,0:T(8,128)(2,1)} custom-call(bf16[32,1024]{1,0:T(8,128)(2,1)} %env_ref.1, s32[1,32]{1,0:T(1,128)} %bitcast.10), custom_call_target="tpu_custom_call" | custom-call | tf_op jit(solution)/shard_map/pack/pallas_call | solution.py:338
  1.5 3.0 %collective-permute-start.3 = (bf16[272,128]{1,0:T(8,128)(2,1)}, bf16[272,128]{1,0:T(8,128)(2,1)S(1)}, u32[]{:S(2)}, u32[]{:S(2)}) collective-permute-start(bf16[272,128]{1,0:T(8,128)(2,1)} %pack.1.own_ref), channel_id=1, source_target_pairs={{0,8},{1,21},{2,10},{3,23},{4,12},{5,17},{6,14},{7,19},{8,0},{9,29... | collective-permute-start | bytes 208904 | tf_op jit(solution)/shard_map/ppermute | solution.py:359
  4.5 1.4 %collective-permute-start.2 = (bf16[272,128]{1,0:T(8,128)(2,1)}, bf16[272,128]{1,0:T(8,128)(2,1)S(1)}, u32[]{:S(2)}, u32[]{:S(2)}) collective-permute-start(bf16[272,128]{1,0:T(8,128)(2,1)} %pack.1.own_ref), channel_id=1, source_target_pairs={{0,12},{1,25},{2,14},{3,27},{4,8},{5,29},{6,10},{7,31},{8,4},{9,17... | collective-permute-start | bytes 208904 | tf_op jit(solution)/shard_map/ppermute | solution.py:359
  5.9 2.6 %collective-permute-start.1 = (bf16[272,128]{1,0:T(8,128)(2,1)}, bf16[272,128]{1,0:T(8,128)(2,1)S(1)}, u32[]{:S(2)}, u32[]{:S(2)}) collective-permute-start(bf16[272,128]{1,0:T(8,128)(2,1)} %pack.1.own_ref), channel_id=1, source_target_pairs={{0,16},{1,29},{2,18},{3,31},{4,20},{5,25},{6,22},{7,27},{8,24},{9,... | collective-permute-start | bytes 208904 | tf_op jit(solution)/shard_map/ppermute | solution.py:359
  8.5 2.4 %collective-permute-start = (bf16[272,128]{1,0:T(8,128)(2,1)}, bf16[272,128]{1,0:T(8,128)(2,1)S(1)}, u32[]{:S(2)}, u32[]{:S(2)}) collective-permute-start(bf16[272,128]{1,0:T(8,128)(2,1)} %pack.1.own_ref), channel_id=1, source_target_pairs={{0,4},{2,6},{4,0},{6,2},{8,12},{10,14},{12,8},{14,10},{16,20},{18,... | collective-permute-start | bytes 208904 | tf_op jit(solution)/shard_map/ppermute | solution.py:359
  10.9 0.0 copy-start
  10.9 2.2 %copy-done = bf16[1,2,1024,1024]{3,2,1,0:T(8,128)(2,1)S(1)} copy-done((bf16[1,2,1024,1024]{3,2,1,0:T(8,128)(2,1)S(1)}, bf16[1,2,1024,1024]{3,2,1,0:T(8,128)(2,1)}, u32[]{:S(2)}) %copy-start) | copy-done | bytes 4194328
  13.1 0.0 copy-start.1
  13.1 0.0 copy-start.2
  13.1 0.0 copy-start.3
  13.1 1.2 %spread.1.prop = bf16[8,2048,128]{2,1,0:T(8,128)(2,1)S(1)} custom-call(bf16[2048,1024]{1,0:T(8,128)(2,1)S(1)} %bitcast.5), custom_call_target="tpu_custom_call" | custom-call | bytes 8388608 | tf_op jit(solution)/shard_map/spread/pallas_call | solution.py:360
  14.3 0.0 collective-permute-done.3
  14.3 0.0 collective-permute-done.2
  14.3 0.0 collective-permute-done.1
  14.3 0.6 %collective-permute-done = bf16[272,128]{1,0:T(8,128)(2,1)S(1)} collective-permute-done((bf16[272,128]{1,0:T(8,128)(2,1)}, bf16[272,128]{1,0:T(8,128)(2,1)S(1)}, u32[]{:S(2)}, u32[]{:S(2)}) %collective-permute-start) | collective-permute-done | bytes 69664 | tf_op jit(solution)/shard_map/ppermute | solution.py:359
  14.9 0.1 collective-permute-start.4
  16.3 0.3 collective-permute-done.4.passed_ref
  16.5 0.0 copy-done.1
  16.5 0.0 copy-done.2
  16.6 0.0 copy-done.3
  16.6 17.7 %propagate.1 = f32[256,128]{1,0:T(8,128)S(1)} custom-call(s32[24,32]{1,0:T(8,128)S(1)} %bitcast.8, f32[1]{0:T(128)S(6)} %copy.8.wavenumber_smem, f32[1]{0:T(128)S(6)} %copy.9.loss_smem, s32[24,32]{1,0:T(8,128)S(1)} %bitcast.9, bf16[64,1024]{1,0:T(8,128)(2,1)S(1)} %bitcast.7, bf16[8,2048,128]{2,1,0:T(8,128)(2,1)S(1)} %spread.1.prop, ...), custom_call_target="tpu_custom_call" | custom-call | tf_op jit(solution)/shard_map/propagate/pallas_call | solution.py:375
  34.2 11.4 %all_to_all.5.parts_ref = f32[32,8,128]{2,1,0:T(8,128)} all-to-all(f32[32,8,128]{2,1,0:T(8,128)S(1)} %bitcast.6), channel_id=1, replica_groups=mesh['bearing'=8,'freq'=4] {'bearing','freq'}, dimensions={0} | all-to-all | bytes 262144 | tf_op jit(solution)/shard_map/all_to_all | solution.py:395
  45.7 1.7 %finish.1 = f32[8,128]{1,0:T(8,128)} custom-call(f32[32,8,128]{2,1,0:T(8,128)} %all_to_all.5.parts_ref), custom_call_target="tpu_custom_call" | custom-call | tf_op jit(solution)/shard_map/finish/pallas_call | solution.py:399
  (1 shorter events, 0.0 us)
Async XLA Ops:
  1.5 12.8 %collective-permute-start.3 = (bf16[272,128]{1,0:T(8,128)(2,1)}, bf16[272,128]{1,0:T(8,128)(2,1)S(1)}, u32[]{:S(2)}, u32[]{:S(2)}) collective-permute-start(bf16[272,128]{1,0:T(8,128)(2,1)} %pack.1.own_ref), channel_id=1, source_target_pairs={{0,8},{1,21},{2,10},{3,23},{4,12},{5,17},{6,14},{7,19},{8,0},{9,29... | collective-permute-start | bytes 208904 | tf_op jit(solution)/shard_map/ppermute | solution.py:359
  4.5 9.8 %collective-permute-start.2 = (bf16[272,128]{1,0:T(8,128)(2,1)}, bf16[272,128]{1,0:T(8,128)(2,1)S(1)}, u32[]{:S(2)}, u32[]{:S(2)}) collective-permute-start(bf16[272,128]{1,0:T(8,128)(2,1)} %pack.1.own_ref), channel_id=1, source_target_pairs={{0,12},{1,25},{2,14},{3,27},{4,8},{5,29},{6,10},{7,31},{8,4},{9,17... | collective-permute-start | bytes 208904 | tf_op jit(solution)/shard_map/ppermute | solution.py:359
  5.9 8.4 %collective-permute-start.1 = (bf16[272,128]{1,0:T(8,128)(2,1)}, bf16[272,128]{1,0:T(8,128)(2,1)S(1)}, u32[]{:S(2)}, u32[]{:S(2)}) collective-permute-start(bf16[272,128]{1,0:T(8,128)(2,1)} %pack.1.own_ref), channel_id=1, source_target_pairs={{0,16},{1,29},{2,18},{3,31},{4,20},{5,25},{6,22},{7,27},{8,24},{9,... | collective-permute-start | bytes 208904 | tf_op jit(solution)/shard_map/ppermute | solution.py:359
  8.5 6.4 %collective-permute-start = (bf16[272,128]{1,0:T(8,128)(2,1)}, bf16[272,128]{1,0:T(8,128)(2,1)S(1)}, u32[]{:S(2)}, u32[]{:S(2)}) collective-permute-start(bf16[272,128]{1,0:T(8,128)(2,1)} %pack.1.own_ref), channel_id=1, source_target_pairs={{0,4},{2,6},{4,0},{6,2},{8,12},{10,14},{12,8},{14,10},{16,20},{18,... | collective-permute-start | bytes 208904 | tf_op jit(solution)/shard_map/ppermute | solution.py:359
  10.9 2.2 %copy-start = (bf16[1,2,1024,1024]{3,2,1,0:T(8,128)(2,1)S(1)}, bf16[1,2,1024,1024]{3,2,1,0:T(8,128)(2,1)}, u32[]{:S(2)}) copy-start(bf16[1,2,1024,1024]{3,2,1,0:T(8,128)(2,1)} %param.8) | copy-start | bytes 12582916
  13.1 3.4 %copy-start.1 = (bf16[272,128]{1,0:T(8,128)(2,1)S(1)}, bf16[272,128]{1,0:T(8,128)(2,1)}, u32[]{:S(2)}) copy-start(bf16[272,128]{1,0:T(8,128)(2,1)} %pack.1.own_ref) | copy-start | bytes 208900
  13.1 3.4 %copy-start.2 = (bf16[1,2,32,1024]{3,2,1,0:T(8,128)(2,1)S(1)}, bf16[1,2,32,1024]{3,2,1,0:T(8,128)(2,1)}, u32[]{:S(2)}) copy-start(bf16[1,2,32,1024]{3,2,1,0:T(8,128)(2,1)} %param.7) | copy-start | bytes 393220
  13.1 3.4 %copy-start.3 = (s32[32,24]{0,1:T(8,128)S(1)}, s32[32,24]{0,1:T(8,128)}, u32[]{:S(2)}) copy-start(s32[32,24]{0,1:T(8,128)} %param.13) | copy-start | bytes 9220
  14.9 1.6 %collective-permute-start.4 = (bf16[1088,128]{1,0:T(8,128)(2,1)S(1)}, bf16[1088,128]{1,0:T(8,128)(2,1)S(1)}, u32[]{:S(2)}, u32[]{:S(2)}) collective-permute-start(bf16[1088,128]{1,0:T(8,128)(2,1)S(1)} %pad_maximum_fusion.direct_ref), channel_id=1, source_target_pairs={{0,1},{1,0},{2,3},{3,2},{4,5},{5,4},{6,7},{7,6},{8,9},{9,8},{10,11... | collective-permute-start | bytes 835592 | tf_op jit(solution)/shard_map/ppermute | solution.py:372
